TPU v7x, 32 devices: a whole 2x2x4 slice. The times are simulated.
32 devices in a mesh: groups: 2 (over y), dp: 8 (over z, x), tensor: 2 (over core).
Axes of the slice: x: 2, y: 2, z: 4, core: 2. Of those that a mesh axis runs over, the one named last changes fastest.
Arguments:
- activations: bfloat16 [96, 48, 4096], P(('groups', 'dp'), None, 'tensor'), parts along dimension 0, may hold values from -6 to 6
- out_grads: bfloat16 [96, 48, 4096], P(('groups', 'dp'), None, 'tensor'), parts along dimension 0, may hold values from -6 to 6
- proj_in: bfloat16 [4096, 64], P('tensor'), may hold values from -0.09375 to 0.09375
- proj_out: bfloat16 [4096, 64], P('tensor'), may hold values from -0.09375 to 0.09375
- queries: bfloat16 [6144, 4096], P(('groups', 'dp', 'tensor')), parts along dimension 0, may hold values from -0.013671875 to 0.013671875
- domains: int32 [96, 2], P(('groups', 'dp')), parts along dimension 0, may hold values from 0 to 7, all different within a row; in each aligned block of 3 rows (0 to 2, 3 to 5, ...) at most 2 rows name the same one
Outputs:
- scores: float32 [96, 2, 384], P(('groups', 'dp', 'tensor')), parts along dimension 0
There are 2 independent parts, one for each index of `groups`. A program takes and returns all parts, laid end to end along the dimension named above; an argument that names none is the same for every part. Nothing has to cross between parts.
Inputs may be any that keep to these rules, and one draw needn't show every extreme that they name: `domains`: each row names 2 different query blocks. In each aligned block of 3 rows no query block is named by more than 2 rows, and some query block is named by exactly 2 rows. The 6 rows of one index of dp span several aligned blocks, so they may name one query block more than 2 times: up to 2 in each aligned block.
All inputs are finite; a program needn't handle non-finite values.
Results may differ from a plain program's by a relative error of at most 0.0029.
Values may be sent and summed in bfloat16 or wider, within the bound.
No kernel may reach another device: no remote copies, remote signals or barrier semaphores. Data moves between devices by JAX's collectives and lax.ppermute only.
A program may use at most 64 MiB of HBM per device.

v0:
```python
import jax
import jax.numpy as jnp
from jax import lax
from jax.sharding import PartitionSpec as P

CAP = 2


def outer_features(proj_grads, proj_acts):
    grams = jnp.einsum("stp,stq->spq", proj_grads, proj_acts, precision=lax.Precision.HIGHEST)
    return grams.reshape(grams.shape[0], -1).astype(jnp.bfloat16)


def body(activations, out_grads, proj_in, proj_out, queries, domains):
    seq_dev, length, in_width = activations.shape
    dp_count = lax.axis_size("dp")
    tensor_count = lax.axis_size("tensor")
    per_share = seq_dev // tensor_count
    proj_acts = jnp.dot(
        activations.reshape(seq_dev * length, in_width), proj_in, preferred_element_type=jnp.float32
    ).reshape(seq_dev, length, -1)
    proj_grads = jnp.dot(
        out_grads.reshape(seq_dev * length, in_width), proj_out, preferred_element_type=jnp.float32
    ).reshape(seq_dev, length, -1)
    proj_acts, proj_grads = lax.psum((proj_acts, proj_grads), "tensor")
    features = outer_features(proj_grads, proj_acts)
    row_count, fanout = domains.shape
    groups = row_count // per_share
    width_out = queries.shape[0]
    per_peer = groups * CAP
    flat_requests = domains.reshape(-1)
    positions = jnp.arange(row_count * fanout, dtype=jnp.int32)
    group_of = positions // fanout // per_share
    slot_keys = group_of * dp_count + flat_requests
    earlier = (slot_keys[None, :] == slot_keys[:, None]) & (positions[None, :] < positions[:, None])
    before_count = jnp.sum(earlier, axis=1, dtype=jnp.int32)
    slot_index = flat_requests * per_peer + group_of * CAP + before_count
    targets = jnp.arange(dp_count * per_peer, dtype=jnp.int32)
    chosen_slots = jnp.any(
        targets[:, None, None] == slot_index.reshape(row_count, fanout)[None, :, :], axis=2
    )
    outgoing = jnp.dot(
        chosen_slots.astype(jnp.bfloat16), features, preferred_element_type=jnp.float32
    )
    outgoing = outgoing.astype(jnp.bfloat16).reshape(dp_count, per_peer, -1)
    scored = lax.dot_general(
        lax.all_to_all(outgoing, "dp", split_axis=0, concat_axis=0, tiled=True),
        queries,
        (((2,), (1,)), ((), ())),
        preferred_element_type=jnp.float32,
    )
    returned = lax.all_to_all(scored, "dp", split_axis=0, concat_axis=0, tiled=True)
    result = jnp.take(returned.reshape(dp_count * per_peer, width_out), slot_index, axis=0)
    result = result.reshape(row_count, fanout, width_out)
    result = lax.all_to_all(result, "tensor", split_axis=0, concat_axis=2, tiled=True)
    return result


def solution(mesh):
    placed = (
        P(("groups", "dp"), None, "tensor"),
        P(("groups", "dp"), None, "tensor"),
        P("tensor", None),
        P("tensor", None),
        P(("groups", "dp", "tensor"), None),
        P(("groups", "dp"), None),
    )
    return jax.shard_map(
        body,
        mesh=mesh,
        in_specs=placed,
        out_specs=P(("groups", "dp", "tensor"), None, None),
        check_vma=False,
    )
```

profile of v0, /device:TPU:0, one launch (start us, length us, event | category | flops | bytes accessed | tf_op | source)
XLA Modules:
  0.0 72.8 jit_solution(747713217284256451)
XLA Ops:
  6.5 2.6 %fusion.2 = f32[6,48,64]{2,1,0:T(8,128)} fusion(bf16[6,48,2048]{2,1,0:T(8,128)(2,1)} %param.6, bf16[2048,64]{0,1:T(8,128)(2,1)} %param.8), kind=kOutput, calls=%fused_computation.5 | convolution fusion | flops 75497472 | bytes 1515520 | tf_op jit(solution)/shard_map/dot_general | solution.py:19
  9.1 1.1 %fusion.4 = f32[6,48,64]{2,1,0:T(8,128)} fusion(bf16[6,48,2048]{2,1,0:T(8,128)(2,1)S(1)} %copy-done.1, bf16[2048,64]{0,1:T(8,128)(2,1)S(1)} %copy-done.2), kind=kOutput, calls=%fused_computation.7 | convolution fusion | flops 75497472 | bytes 1515520 | tf_op jit(solution)/shard_map/dot_general | solution.py:22
  10.2 0.0 all-reduce.3.cloned.1.call-update
  10.3 0.1 copy.21
  10.4 0.1 reshape.206
  10.5 0.2 convert_reduce_fusion
  10.7 0.1 reduce_sum.14
  10.8 0.1 copy.23
  10.9 0.1 fusion.7
  10.9 20.6 %all-reduce.3.cloned.1.call-done = (f32[6,48,64]{2,1,0:T(8,128)}, f32[6,48,64]{2,1,0:T(8,128)}) async-done(((f32[6,48,64]{2,1,0:T(8,128)}, f32[6,48,64]{2,1,0:T(8,128)}), (f32[6,48,64]{2,1,0:T(8,128)}, f32[6,48,64]{2,1,0:T(8,128)})) %all-reduce.3.cloned.1.call-update) | async-done | bytes 147472 | tf_op jit(solution)/shard_map/psum | solution.py:25
  31.5 1.5 %convolution_convert_fusion.1 = bf16[6,64,64]{2,1,0:T(8,128)(2,1)S(1)} fusion(f32[6,48,64]{2,1,0:T(8,128)} %get-tuple-element.5, f32[6,48,64]{2,1,0:T(8,128)} %get-tuple-element.6), kind=kOutput, calls=%fused_computation.4 | convolution fusion | flops 14180352 | bytes 196608 | tf_op jit(solution)/shard_map/stp,stq->spq/dot_general | solution.py:10
  33.0 0.1 convert_element_type.15
  33.1 0.3 convolution_convert_fusion
  33.4 0.8 %reshape.207 = bf16[8,4,4096]{2,1,0:T(4,128)(2,1)} reshape(bf16[32,4096]{1,0:T(8,128)(2,1)S(1)} %convolution_convert_fusion) | data formatting | bytes 524288 | tf_op jit(solution)/shard_map/reshape | solution.py:45
  34.2 5.8 %all-to-all-start = ((bf16[8,4,4096]{2,1,0:T(4,128)(2,1)}), bf16[8,4,4096]{2,1,0:T(4,128)(2,1)S(1)}, u32[]{:S(2)}, u32[]{:S(2)}) async-start(bf16[8,4,4096]{2,1,0:T(4,128)(2,1)} %reshape.207), calls=%async_computation | async-start | bytes 524288 | tf_op jit(solution)/shard_map/all_to_all | solution.py:47
  40.0 0.1 mul.52
  40.1 9.2 %all-to-all-done = bf16[8,4,4096]{2,1,0:T(4,128)(2,1)S(1)} async-done(((bf16[8,4,4096]{2,1,0:T(4,128)(2,1)}), bf16[8,4,4096]{2,1,0:T(4,128)(2,1)S(1)}, u32[]{:S(2)}, u32[]{:S(2)}) %all-to-all-start) | async-done | bytes 262176 | tf_op jit(solution)/shard_map/all_to_all | solution.py:47
  49.4 1.2 %fusion = f32[8,4,192]{2,1,0:T(4,128)} fusion(bf16[8,4,4096]{2,1,0:T(4,128)(2,1)S(1)} %all-to-all-done, bf16[192,4096]{1,0:T(8,128)(2,1)S(1)} %copy-done), kind=kOutput, calls=%fused_computation.2 | convolution fusion | flops 50331648 | bytes 1859584 | tf_op jit(solution)/shard_map/dot_general | solution.py:46
  50.6 3.6 %all-to-all-start.1 = ((f32[8,4,192]{2,1,0:T(4,128)}), f32[8,4,192]{2,1,0:T(4,128)S(1)}, u32[]{:S(2)}, u32[]{:S(2)}) async-start(f32[8,4,192]{2,1,0:T(4,128)} %fusion), calls=%async_computation.1 | async-start | bytes 65536 | tf_op jit(solution)/shard_map/all_to_all | solution.py:52
  54.2 6.7 %all-to-all-done.1 = f32[8,4,192]{2,1,0:T(4,128)S(1)} async-done(((f32[8,4,192]{2,1,0:T(4,128)}), f32[8,4,192]{2,1,0:T(4,128)S(1)}, u32[]{:S(2)}, u32[]{:S(2)}) %all-to-all-start.1) | async-done | bytes 24608 | tf_op jit(solution)/shard_map/all_to_all | solution.py:52
  60.9 0.6 gather_fusion
  61.5 0.1 broadcast_select_fusion
  61.5 3.7 %all_to_all.28 = f32[6,2,192]{2,1,0:T(2,128)S(1)} all-to-all(f32[6,2,192]{2,1,0:T(2,128)S(1)} %broadcast_select_fusion), channel_id=1, replica_groups=mesh['groups'=2,'dp'=8,'tensor'=2] {'tensor'}, dimensions={0} | all-to-all | bytes 18432 | tf_op jit(solution)/shard_map/all_to_all | solution.py:55
  65.3 0.7 all_to_all.24
  (17 shorter events, 0.2 us)
Async XLA Ops:
  6.5 42.8 %copy-start = (bf16[192,4096]{1,0:T(8,128)(2,1)S(1)}, bf16[192,4096]{1,0:T(8,128)(2,1)}, u32[]{:S(2)}) copy-start(bf16[192,4096]{1,0:T(8,128)(2,1)} %param.10) | copy-start | bytes 4718596
  6.5 2.6 %copy-start.2 = (bf16[2048,64]{0,1:T(8,128)(2,1)S(1)}, bf16[2048,64]{0,1:T(8,128)(2,1)}, u32[]{:S(2)}) copy-start(bf16[2048,64]{0,1:T(8,128)(2,1)} %param.9) | copy-start | bytes 786436
  6.5 2.6 %copy-start.1 = (bf16[6,48,2048]{2,1,0:T(8,128)(2,1)S(1)}, bf16[6,48,2048]{2,1,0:T(8,128)(2,1)}, u32[]{:S(2)}) copy-start(bf16[6,48,2048]{2,1,0:T(8,128)(2,1)} %param.7) | copy-start | bytes 3538948
  6.5 24.9 %all-reduce.3.cloned.1.call-start = ((), (), s32[]{:S(2)}) async-start(), calls=%async_computation.3 | async-start | bytes 589824 | tf_op jit(solution)/shard_map/psum | solution.py:25
  9.1 1.1 %copy-start.3 = (s32[6,2]{0,1:T(2,128)S(1)}, s32[6,2]{0,1:T(2,128)}, u32[]{:S(2)}) copy-start(s32[6,2]{0,1:T(2,128)} %param.11) | copy-start | bytes 148
  34.2 15.2 %all-to-all-start = ((bf16[8,4,4096]{2,1,0:T(4,128)(2,1)}), bf16[8,4,4096]{2,1,0:T(4,128)(2,1)S(1)}, u32[]{:S(2)}, u32[]{:S(2)}) async-start(bf16[8,4,4096]{2,1,0:T(4,128)(2,1)} %reshape.207), calls=%async_computation | async-start | bytes 524288 | tf_op jit(solution)/shard_map/all_to_all | solution.py:47
  50.6 10.3 %all-to-all-start.1 = ((f32[8,4,192]{2,1,0:T(4,128)}), f32[8,4,192]{2,1,0:T(4,128)S(1)}, u32[]{:S(2)}, u32[]{:S(2)}) async-start(f32[8,4,192]{2,1,0:T(4,128)} %fusion), calls=%async_computation.1 | async-start | bytes 65536 | tf_op jit(solution)/shard_map/all_to_all | solution.py:52
Sparse Core Ops, SparseCore 0:
  10.4 21.0 all-reduce.2
where the time goes:
time: 73.1 us; the launch traced here: 72.8 us
  waiting for transfers between devices  36.5 us (50%)
  between operations  13.5 us (18%)
  starting transfers between devices  9.36 us (13%)
  matrix products  6.67 us (9%)
  blocking collectives  3.71 us (5%)
  local copies, waits for them, and re-layouts  2.67 us (4%)
    psum x1, waiting for transfers between devices, body(): proj_acts, proj_grads = lax.psum((proj_acts, proj_grads), 'tensor')  20.6 us
    all_to_all x1, waiting for transfers between devices, body(): lax.all_to_all(outgoing, 'dp', split_axis=0, concat_axis=0, tiled=True)  9.25 us
    all_to_all x1, waiting for transfers between devices, body(): lax.all_to_all(scored, 'dp', split_axis=0, concat_axis=0, tiled=True)  6.68 us
    all_to_all x1, starting transfers between devices, body(): lax.all_to_all(outgoing, 'dp', split_axis=0, concat_axis=0, tiled=True)  5.77 us
    all_to_all x1, blocking collectives, body(): lax.all_to_all(result, 'tensor', split_axis=0, concat_axis=2, tiled=True)  3.71 us
    all_to_all x1, starting transfers between devices, body(): lax.all_to_all(scored, 'dp', split_axis=0, concat_axis=0, tiled=True)  3.59 us
    dot_general x1, matrix products, body(): jnp.dot(activations.reshape(seq_dev * length, in_width), proj_in, preferr...  2.57 us
    dot_general x1, matrix products, outer_features(): jnp.einsum('stp,stq->spq', proj_grads, proj_acts, precision=lax.Precision...  1.49 us
  transfers between devices with their start and end apart: 3, of which 3 were waited for; matrix products, arithmetic and copies ran while one was open for 1% of the time, Pallas kernels for 0%

commit v1 on v0

v1 whole, which is shorter than its diff:
```python
import functools

import jax
import jax.numpy as jnp
from jax import lax
from jax.experimental import pallas as pl
from jax.experimental.pallas import tpu as pltpu
from jax.sharding import PartitionSpec as P

CAP = 2
CHUNKS = 4
LANES = 128

VMEM = pl.BlockSpec(memory_space=pltpu.VMEM)
SMEM = pl.BlockSpec(memory_space=pltpu.SMEM)
ANY = pl.BlockSpec(memory_space=pl.ANY)


def each(count, step):
    if count <= 8:
        for at in range(count):
            step(at)
    else:
        lax.fori_loop(0, count, lambda at, _: (step(at), 0)[1], 0)


def project_kernel(acts, grads, p_in, p_out, out, acts_v, grads_v, in_v, out_v, sems):
    width = acts.shape[1]
    size = width // CHUNKS
    copies = []
    for side, (x, x_v, w, w_v) in enumerate(((acts, acts_v, p_in, in_v), (grads, grads_v, p_out, out_v))):
        for c in range(CHUNKS):
            part = pl.ds(c * size, size)
            copies.append(
                (
                    pltpu.make_async_copy(w.at[part], w_v.at[part], sems.at[side, c, 0]),
                    pltpu.make_async_copy(x.at[:, part], x_v.at[c], sems.at[side, c, 1]),
                )
            )
    for pair in copies:
        for copy in pair:
            copy.start()
    sums = []
    for side, (x_v, w_v) in enumerate(((acts_v, in_v), (grads_v, out_v))):
        total = None
        for c in range(CHUNKS):
            for copy in copies[side * CHUNKS + c]:
                copy.wait()
            term = jnp.dot(x_v[c], w_v[pl.ds(c * size, size)], preferred_element_type=jnp.float32)
            total = term if total is None else total + term
        sums.append(total)
    out[...] = jnp.concatenate(sums, axis=1)


def project(acts, grads, p_in, p_out):
    rows, width = acts.shape
    proj = p_in.shape[1]
    return pl.pallas_call(
        project_kernel,
        out_shape=jax.ShapeDtypeStruct((rows, 2 * proj), jnp.float32),
        in_specs=[ANY] * 4,
        out_specs=VMEM,
        scratch_shapes=[
            pltpu.VMEM((CHUNKS, rows, width // CHUNKS), jnp.bfloat16),
            pltpu.VMEM((CHUNKS, rows, width // CHUNKS), jnp.bfloat16),
            pltpu.VMEM((width, proj), jnp.bfloat16),
            pltpu.VMEM((width, proj), jnp.bfloat16),
            pltpu.SemaphoreType.DMA((2, CHUNKS, 2)),
        ],
        name="project",
    )(acts, grads, p_in, p_out)


def rank(domains, row, first, named):
    fanout = domains.shape[1]
    found = jnp.int32(0)
    for other in range(first, row):
        if fanout <= 8:
            for k in range(fanout):
                found += (domains[other, k] == named).astype(jnp.int32)
        else:
            found = lax.fori_loop(
                0, fanout, lambda k, n, other=other: n + (domains[other, k] == named).astype(jnp.int32), found
            )
    return found


def feature_kernel(share, domains, own, other, out, grams):
    seqs, fanout = domains.shape
    length = own.shape[0] // seqs
    proj = own.shape[1] // 2
    half = out.shape[2]
    out[...] = jnp.zeros_like(out)
    both = own[...] + other[...]
    high = both.astype(jnp.bfloat16)
    low = (both - high.astype(jnp.float32)).astype(jnp.bfloat16)
    mine = proj + lax.axis_index("tensor") * 2 * half
    left = lax.broadcasted_iota(jnp.int32, (half, LANES), 1) < proj
    for s in range(seqs):
        at = slice(s * length, (s + 1) * length)
        h, l = high[at], low[at]
        grams[s] = lax.dot_general(
            jnp.concatenate([h, l, h], axis=0),
            jnp.concatenate([h, h, l], axis=0),
            (((0,), (0,)), ((), ())),
            preferred_element_type=jnp.float32,
        )
    for s in range(seqs):
        even = grams[s, pl.ds(mine, half, stride=2), :]
        odd = grams[s, pl.ds(mine + 1, half, stride=2), :]
        feature = jnp.where(left, even, pltpu.roll(odd, proj, 1)).astype(out.dtype)
        group = s // share

        def place(k, s=s, group=group, feature=feature):
            named = domains[s, k]
            out[named, group * CAP + rank(domains, s, group * share, named)] = feature

        each(fanout, place)


def spread(domains, own, other, share, peers, tensor_count):
    seqs = domains.shape[0]
    proj = own.shape[1] // 2
    half = proj * proj // LANES // tensor_count
    return pl.pallas_call(
        functools.partial(feature_kernel, share),
        out_shape=jax.ShapeDtypeStruct((peers, seqs // share * CAP, half, LANES), jnp.bfloat16),
        in_specs=[SMEM, VMEM, VMEM],
        out_specs=VMEM,
        scratch_shapes=[pltpu.VMEM((seqs, 2 * proj, 2 * proj), jnp.float32)],
        name="spread",
    )(domains, own, other)


def score_kernel(features, own, other, out, rows_v):
    peers, slots, half, _ = features.shape
    count = peers * slots
    rows_v[...] = features[...].reshape(count * half, LANES).astype(jnp.float32)
    rows = jnp.concatenate(
        [rows_v[pl.ds(c, count, stride=half), :].astype(jnp.bfloat16) for c in range(half)], axis=1
    )
    me = lax.axis_index("tensor")
    part = pl.ds(pl.multiple_of(me * half * LANES, LANES), half * LANES)
    mine, theirs = (
        lax.dot_general(rows, q[:, part], (((1,), (1,)), ((), ())), preferred_element_type=jnp.float32)
        for q in (own, other)
    )
    scores = jnp.concatenate([jnp.where(me == 0, mine, theirs), jnp.where(me == 0, theirs, mine)], axis=1)
    for p in range(out.shape[0]):
        out[p] = scores[p * CAP : (p + 1) * CAP]


def score(features, own, other):
    peers, slots, half, _ = features.shape
    return pl.pallas_call(
        score_kernel,
        out_shape=jax.ShapeDtypeStruct((peers * slots // CAP, CAP, 2 * own.shape[0]), jnp.float32),
        in_specs=[VMEM] * 3,
        out_specs=VMEM,
        scratch_shapes=[pltpu.VMEM((peers * slots * half, LANES), jnp.float32)],
        name="score",
    )(features, own, other)


def pick_kernel(domains, scores, out):
    share, fanout, _ = out.shape
    first = lax.axis_index("tensor") * share
    for s in range(share):

        def take(k, s=s):
            named = domains[first + s, k]
            found = jnp.int32(0)
            for other in range(s):
                found += sum((domains[first + other, j] == named).astype(jnp.int32) for j in range(fanout))
            both = scores[2 * named] + scores[2 * named + 1]
            out[s, pl.ds(k, 1)] = jnp.where(found == 0, both[0:1], both[1:2])

        each(fanout, take)


def pick(domains, scores, share):
    return pl.pallas_call(
        pick_kernel,
        out_shape=jax.ShapeDtypeStruct((share, domains.shape[1], scores.shape[2]), jnp.float32),
        in_specs=[SMEM, VMEM],
        out_specs=VMEM,
        name="pick",
    )(domains, scores)


def body(activations, out_grads, proj_in, proj_out, queries, domains):
    seqs, length, width = activations.shape
    peers = lax.axis_size("dp")
    tensor_count = lax.axis_size("tensor")
    share = seqs // tensor_count
    swap = [(i, i ^ 1) for i in range(tensor_count)]
    own = project(
        activations.reshape(seqs * length, width), out_grads.reshape(seqs * length, width), proj_in, proj_out
    )
    other = lax.ppermute(own, "tensor", swap)
    other_queries = lax.ppermute(queries, "tensor", swap)
    sent = spread(domains, own, other, share, peers, tensor_count)
    came = lax.all_to_all(sent, "dp", split_axis=0, concat_axis=0, tiled=True)
    scores = score(came, queries, other_queries)
    back = lax.all_to_all(scores, ("dp", "tensor"), split_axis=0, concat_axis=0, tiled=True)
    return pick(domains, back, share)


def solution(mesh):
    placed = (
        P(("groups", "dp"), None, "tensor"),
        P(("groups", "dp"), None, "tensor"),
        P("tensor", None),
        P("tensor", None),
        P(("groups", "dp", "tensor"), None),
        P(("groups", "dp"), None),
    )
    return jax.shard_map(
        body,
        mesh=mesh,
        in_specs=placed,
        out_specs=P(("groups", "dp", "tensor"), None, None),
        check_vma=False,
    )
```

time: 73.1 us -> 44.1 us (0.60)
  waiting for transfers between devices: 36.5 us -> 0.85 us
  blocking collectives: 3.71 us -> 25.5 us
  between operations: 13.5 us -> 0.02 us
  Pallas kernels: 0 us -> 10.4 us
  starting transfers between devices: 9.36 us -> 0.58 us
  matrix products: 6.67 us -> 0 us
  local copies, waits for them, and re-layouts: 2.67 us -> 6.41 us
    all_to_all x1 -> x2, blocking collectives: 3.71 us -> 25.5 us  [the longest x1 14.6 us: body(): came = lax.all_to_all(sent, 'dp', split_axis=0, concat_axis=0, tiled=True)]
    psum x1 -> x0, waiting for transfers between devices: 20.6 us -> none  [body(): proj_acts, proj_grads = lax.psum((proj_acts, proj_grads), 'tensor')]
    all_to_all x2 -> x0, waiting for transfers between devices: 15.9 us -> none  [the longest x1 9.25 us: body(): lax.all_to_all(outgoing, 'dp', split_axis=0, concat_axis=0, tiled=True)]
    pallas_call x0 -> x4, Pallas kernels: none -> 10.4 us  [the longest x1 3.74 us: project(): pl.pallas_call(project_kernel, out_shape=jax.ShapeDtypeStruct((rows, 2 *...]
    all_to_all x2 -> x0, starting transfers between devices: 9.36 us -> none  [the longest x1 5.77 us: body(): lax.all_to_all(outgoing, 'dp', split_axis=0, concat_axis=0, tiled=True)]
    dot_general x5 -> x0, matrix products: 6.67 us -> none  [the longest x1 2.57 us: body(): jnp.dot(activations.reshape(seq_dev * length, in_width), proj_in, preferr...]
    unnamed x9, local copies, waits for them, and re-layouts: 0.11 us -> 6.41 us
    reshape x3 -> x0, local copies, waits for them, and re-layouts: 0.9 us -> none  [the longest x1 0.8 us: body(): outgoing = outgoing.astype(jnp.bfloat16).reshape(dp_count, per_peer, -1)]
  transfers between devices with their start and end apart: 3 -> 2, of which waited for: 3 -> 1; matrix products, arithmetic and copies ran while one was open for 1% -> 11% of each run, Pallas kernels for 0% -> 13%
where the time goes in v1:
time: 44.1 us; the launch traced here: 43.7 us
  blocking collectives  25.5 us (58%)
  Pallas kernels  10.4 us (24%)
  local copies, waits for them, and re-layouts  6.41 us (15%)
  waiting for transfers between devices  0.85 us (2%)
  starting transfers between devices  0.58 us (1%)
    all_to_all x1, blocking collectives, body(): came = lax.all_to_all(sent, 'dp', split_axis=0, concat_axis=0, tiled=True)  14.6 us
    all_to_all x1, blocking collectives, body(): lax.all_to_all(scores, ('dp', 'tensor'), split_axis=0, concat_axis=0, til...  10.9 us
    unnamed x9, local copies, waits for them, and re-layouts  6.41 us
    pallas_call x1, Pallas kernels, project(): pl.pallas_call(project_kernel, out_shape=jax.ShapeDtypeStruct((rows, 2 *...  3.74 us
    pallas_call x1, Pallas kernels, score(): pl.pallas_call(score_kernel, out_shape=jax.ShapeDtypeStruct((peers * slot...  3.22 us
    pallas_call x1, Pallas kernels, spread(): pl.pallas_call(functools.partial(feature_kernel, share), out_shape=jax.Sh...  2.03 us
    pallas_call x1, Pallas kernels, pick(): pl.pallas_call(pick_kernel, out_shape=jax.ShapeDtypeStruct((share, domain...  1.44 us
  transfers between devices with their start and end apart: 2, of which 1 were waited for; matrix products, arithmetic and copies ran while one was open for 11% of the time, Pallas kernels for 13%

profile of v1, /device:TPU:0, one launch (start us, length us, event | category | flops | bytes accessed | tf_op | source)
XLA Modules:
  0.0 43.7 jit_solution(3187886374469094258)
XLA Ops:
  0.0 0.5 %collective-permute-start.1 = (bf16[192,4096]{1,0:T(8,128)(2,1)}, bf16[192,4096]{1,0:T(8,128)(2,1)S(1)}, u32[]{:S(2)}, u32[]{:S(2)}) collective-permute-start(bf16[192,4096]{1,0:T(8,128)(2,1)} %own.1), channel_id=1, source_target_pairs={{0,1},{1,0},{2,3},{3,2},{4,5},{5,4},{6,7},{7,6},{8,9},{9,8},{10,11... | collective-permute-start | bytes 4718600 | tf_op jit(solution)/shard_map/ppermute | solution.py:201
  0.5 2.0 %copy.7.p_in = bf16[2048,64]{1,0:T(8,128)(2,1)} copy(bf16[2048,64]{0,1:T(8,128)(2,1)} %param.8) | data formatting | bytes 524288 | tf_op args[2]
  2.4 2.0 %copy.8.p_out = bf16[2048,64]{1,0:T(8,128)(2,1)} copy(bf16[2048,64]{0,1:T(8,128)(2,1)} %param.9) | data formatting | bytes 524288 | tf_op args[3]
  4.4 0.0 copy-start.2
  4.4 3.7 %project.1.own = f32[288,128]{1,0:T(8,128)} custom-call(bf16[288,2048]{1,0:T(8,128)(2,1)} %bitcast.2, bf16[288,2048]{1,0:T(8,128)(2,1)} %bitcast.3, bf16[2048,64]{1,0:T(8,128)(2,1)} %copy.7.p_in, bf16[2048,64]{1,0:T(8,128)(2,1)} %copy.8.p_out), custom_call_target="tpu_custom_call" | custom-call | tf_op jit(solution)/shard_map/project/pallas_call | solution.py:58
  8.1 0.1 collective-permute-start
  8.2 0.0 copy-done.2
  8.2 0.7 %copy.10.domains = s32[6,2]{1,0:T(8,128)} copy(s32[6,2]{0,1:T(2,128)S(1)} %copy-done.2) | data formatting | bytes 96 | tf_op args[5]
  8.9 0.8 %collective-permute-done.other = f32[288,128]{1,0:T(8,128)S(1)} collective-permute-done((f32[288,128]{1,0:T(8,128)}, f32[288,128]{1,0:T(8,128)S(1)}, u32[]{:S(2)}, u32[]{:S(2)}) %collective-permute-start) | collective-permute-done | bytes 147488 | tf_op jit(solution)/shard_map/ppermute | solution.py:200
  9.8 0.0 copy-start.1
  9.8 0.7 %copy-done.1 = f32[288,128]{1,0:T(8,128)} copy-done((f32[288,128]{1,0:T(8,128)}, f32[288,128]{1,0:T(8,128)S(1)}, u32[]{:S(2)}) %copy-start.1) | copy-done | bytes 147480
  10.4 2.0 %spread.1 = bf16[8,4,16,128]{3,2,1,0:T(8,128)(2,1)} custom-call(s32[6,2]{1,0:T(8,128)} %copy.10.domains, f32[288,128]{1,0:T(8,128)} %project.1.own, f32[288,128]{1,0:T(8,128)} %copy-done.1), custom_call_target="tpu_custom_call" | custom-call | tf_op jit(solution)/shard_map/spread/pallas_call | solution.py:125
  12.4 14.6 %all_to_all.10.features = bf16[8,4,16,128]{3,2,1,0:T(8,128)(2,1)} all-to-all(bf16[8,4,16,128]{3,2,1,0:T(8,128)(2,1)} %spread.1), channel_id=1, replica_groups=mesh['groups'=2,'dp'=8,'tensor'=2] {'dp'}, dimensions={0} | all-to-all | bytes 262144 | tf_op jit(solution)/shard_map/all_to_all | solution.py:203
  27.0 0.0 collective-permute-done.1.other
  27.0 0.0 copy-start
  27.0 1.2 %copy-done = bf16[192,4096]{1,0:T(8,128)(2,1)} copy-done((bf16[192,4096]{1,0:T(8,128)(2,1)}, bf16[192,4096]{1,0:T(8,128)(2,1)S(1)}, u32[]{:S(2)}) %copy-start) | copy-done | bytes 1572888
  28.2 3.2 %score.1 = f32[16,2,384]{2,1,0:T(2,128)} custom-call(bf16[8,4,16,128]{3,2,1,0:T(8,128)(2,1)} %all_to_all.10.features, bf16[192,4096]{1,0:T(8,128)(2,1)} %own.1, bf16[192,4096]{1,0:T(8,128)(2,1)} %copy-done), custom_call_target="tpu_custom_call" | custom-call | tf_op jit(solution)/shard_map/score/pallas_call | solution.py:155
  31.4 10.9 %all_to_all.11.scores = f32[16,2,384]{2,1,0:T(2,128)} all-to-all(f32[16,2,384]{2,1,0:T(2,128)} %score.1), channel_id=1, replica_groups=mesh['groups'=2,'dp'=8,'tensor'=2] {'dp','tensor'}, dimensions={0} | all-to-all | bytes 98304 | tf_op jit(solution)/shard_map/all_to_all | solution.py:205
  42.3 1.4 %pick.1 = f32[3,2,384]{2,1,0:T(2,128)} custom-call(s32[6,2]{1,0:T(8,128)} %copy.10.domains, f32[16,2,384]{2,1,0:T(2,128)} %all_to_all.11.scores), custom_call_target="tpu_custom_call" | custom-call | tf_op jit(solution)/shard_map/pick/pallas_call | solution.py:182
Async XLA Ops:
  0.0 27.0 %collective-permute-start.1 = (bf16[192,4096]{1,0:T(8,128)(2,1)}, bf16[192,4096]{1,0:T(8,128)(2,1)S(1)}, u32[]{:S(2)}, u32[]{:S(2)}) collective-permute-start(bf16[192,4096]{1,0:T(8,128)(2,1)} %own.1), channel_id=1, source_target_pairs={{0,1},{1,0},{2,3},{3,2},{4,5},{5,4},{6,7},{7,6},{8,9},{9,8},{10,11... | collective-permute-start | bytes 4718600 | tf_op jit(solution)/shard_map/ppermute | solution.py:201
  4.4 3.9 %copy-start.2 = (s32[6,2]{0,1:T(2,128)S(1)}, s32[6,2]{0,1:T(2,128)}, u32[]{:S(2)}) copy-start(s32[6,2]{0,1:T(2,128)} %param.11) | copy-start | bytes 148
  8.1 1.6 %collective-permute-start = (f32[288,128]{1,0:T(8,128)}, f32[288,128]{1,0:T(8,128)S(1)}, u32[]{:S(2)}, u32[]{:S(2)}) collective-permute-start(f32[288,128]{1,0:T(8,128)} %project.1.own), channel_id=1, source_target_pairs={{0,1},{1,0},{2,3},{3,2},{4,5},{5,4},{6,7},{7,6},{8,9},{9,8},{10,11... | collective-permute-start | bytes 442376 | tf_op jit(solution)/shard_map/ppermute | solution.py:200
  9.8 0.7 %copy-start.1 = (f32[288,128]{1,0:T(8,128)}, f32[288,128]{1,0:T(8,128)S(1)}, u32[]{:S(2)}) copy-start(f32[288,128]{1,0:T(8,128)S(1)} %collective-permute-done.other) | copy-start | bytes 442372
  27.0 1.2 %copy-start = (bf16[192,4096]{1,0:T(8,128)(2,1)}, bf16[192,4096]{1,0:T(8,128)(2,1)S(1)}, u32[]{:S(2)}) copy-start(bf16[192,4096]{1,0:T(8,128)(2,1)S(1)} %collective-permute-done.1.other) | copy-start | bytes 4718596

commit v2 on v1

--- a/solution.py
+++ b/solution.py
@@ -1,4 +1,5 @@
 import functools
+import math
 
 import jax
 import jax.numpy as jnp
@@ -10,6 +11,7 @@
 CAP = 2
 CHUNKS = 4
 LANES = 128
+LAST = (((1,), (1,)), ((), ()))
 
 VMEM = pl.BlockSpec(memory_space=pltpu.VMEM)
 SMEM = pl.BlockSpec(memory_space=pltpu.SMEM)
@@ -22,6 +24,11 @@
             step(at)
     else:
         lax.fori_loop(0, count, lambda at, _: (step(at), 0)[1], 0)
+
+
+def room(*shapes):
+    held = sum(math.prod(shape) * jnp.dtype(dtype).itemsize for shape, dtype in shapes)
+    return pltpu.CompilerParams(vmem_limit_bytes=2 * held + (1 << 20))
 
 
 def project_kernel(acts, grads, p_in, p_out, out, acts_v, grads_v, in_v, out_v, sems):
@@ -33,7 +40,7 @@
             part = pl.ds(c * size, size)
             copies.append(
                 (
-                    pltpu.make_async_copy(w.at[part], w_v.at[part], sems.at[side, c, 0]),
+                    pltpu.make_async_copy(w.at[:, part], w_v.at[:, part], sems.at[side, c, 0]),
                     pltpu.make_async_copy(x.at[:, part], x_v.at[c], sems.at[side, c, 1]),
                 )
             )
@@ -46,7 +53,7 @@
         for c in range(CHUNKS):
             for copy in copies[side * CHUNKS + c]:
                 copy.wait()
-            term = jnp.dot(x_v[c], w_v[pl.ds(c * size, size)], preferred_element_type=jnp.float32)
+            term = lax.dot_general(x_v[c], w_v[:, pl.ds(c * size, size)], LAST, preferred_element_type=jnp.float32)
             total = term if total is None else total + term
         sums.append(total)
     out[...] = jnp.concatenate(sums, axis=1)
@@ -54,7 +61,8 @@
 
 def project(acts, grads, p_in, p_out):
     rows, width = acts.shape
-    proj = p_in.shape[1]
+    proj = p_in.shape[0]
+    bf16 = jnp.bfloat16
     return pl.pallas_call(
         project_kernel,
         out_shape=jax.ShapeDtypeStruct((rows, 2 * proj), jnp.float32),
@@ -63,30 +71,31 @@
         scratch_shapes=[
             pltpu.VMEM((CHUNKS, rows, width // CHUNKS), jnp.bfloat16),
             pltpu.VMEM((CHUNKS, rows, width // CHUNKS), jnp.bfloat16),
-            pltpu.VMEM((width, proj), jnp.bfloat16),
-            pltpu.VMEM((width, proj), jnp.bfloat16),
+            pltpu.VMEM((proj, width), jnp.bfloat16),
+            pltpu.VMEM((proj, width), jnp.bfloat16),
             pltpu.SemaphoreType.DMA((2, CHUNKS, 2)),
         ],
+        compiler_params=room((acts.shape, bf16), (p_in.shape, bf16), ((rows, 2 * LANES), jnp.float32)),
         name="project",
     )(acts, grads, p_in, p_out)
 
 
 def rank(domains, row, first, named):
-    fanout = domains.shape[1]
+    fanout = domains.shape[0]
     found = jnp.int32(0)
     for other in range(first, row):
         if fanout <= 8:
             for k in range(fanout):
-                found += (domains[other, k] == named).astype(jnp.int32)
+                found += (domains[k, other] == named).astype(jnp.int32)
         else:
             found = lax.fori_loop(
-                0, fanout, lambda k, n, other=other: n + (domains[other, k] == named).astype(jnp.int32), found
+                0, fanout, lambda k, n, other=other: n + (domains[k, other] == named).astype(jnp.int32), found
             )
     return found
 
 
 def feature_kernel(share, domains, own, other, out, grams):
-    seqs, fanout = domains.shape
+    fanout, seqs = domains.shape
     length = own.shape[0] // seqs
     proj = own.shape[1] // 2
     half = out.shape[2]
@@ -112,14 +121,14 @@
         group = s // share
 
         def place(k, s=s, group=group, feature=feature):
-            named = domains[s, k]
+            named = domains[k, s]
             out[named, group * CAP + rank(domains, s, group * share, named)] = feature
 
         each(fanout, place)
 
 
 def spread(domains, own, other, share, peers, tensor_count):
-    seqs = domains.shape[0]
+    seqs = domains.shape[1]
     proj = own.shape[1] // 2
     half = proj * proj // LANES // tensor_count
     return pl.pallas_call(
@@ -128,6 +137,9 @@
         in_specs=[SMEM, VMEM, VMEM],
         out_specs=VMEM,
         scratch_shapes=[pltpu.VMEM((seqs, 2 * proj, 2 * proj), jnp.float32)],
+        compiler_params=room(
+            ((4 * own.shape[0], LANES), jnp.float32), ((peers, seqs // share * CAP, half, LANES), jnp.bfloat16)
+        ),
         name="spread",
     )(domains, own, other)
 
@@ -142,7 +154,7 @@
     me = lax.axis_index("tensor")
     part = pl.ds(pl.multiple_of(me * half * LANES, LANES), half * LANES)
     mine, theirs = (
-        lax.dot_general(rows, q[:, part], (((1,), (1,)), ((), ())), preferred_element_type=jnp.float32)
+        lax.dot_general(rows, q[:, part], LAST, preferred_element_type=jnp.float32)
         for q in (own, other)
     )
     scores = jnp.concatenate([jnp.where(me == 0, mine, theirs), jnp.where(me == 0, theirs, mine)], axis=1)
@@ -158,6 +170,12 @@
         in_specs=[VMEM] * 3,
         out_specs=VMEM,
         scratch_shapes=[pltpu.VMEM((peers * slots * half, LANES), jnp.float32)],
+        compiler_params=room(
+            (features.shape, jnp.bfloat16),
+            ((peers * slots * half, LANES), jnp.float32),
+            ((2 * own.shape[0], own.shape[1]), jnp.bfloat16),
+            ((peers * slots // CAP, 8, 2 * own.shape[0]), jnp.float32),
+        ),
         name="score",
     )(features, own, other)
 
@@ -168,10 +186,10 @@
     for s in range(share):
 
         def take(k, s=s):
-            named = domains[first + s, k]
+            named = domains[k, first + s]
             found = jnp.int32(0)
             for other in range(s):
-                found += sum((domains[first + other, j] == named).astype(jnp.int32) for j in range(fanout))
+                found += sum((domains[j, first + other] == named).astype(jnp.int32) for j in range(fanout))
             both = scores[2 * named] + scores[2 * named + 1]
             out[s, pl.ds(k, 1)] = jnp.where(found == 0, both[0:1], both[1:2])
 
@@ -181,9 +199,10 @@
 def pick(domains, scores, share):
     return pl.pallas_call(
         pick_kernel,
-        out_shape=jax.ShapeDtypeStruct((share, domains.shape[1], scores.shape[2]), jnp.float32),
+        out_shape=jax.ShapeDtypeStruct((share, domains.shape[0], scores.shape[2]), jnp.float32),
         in_specs=[SMEM, VMEM],
         out_specs=VMEM,
+        compiler_params=room((scores.shape, jnp.float32), ((8 * share, domains.shape[0], scores.shape[2]), jnp.float32)),
         name="pick",
     )(domains, scores)
 
@@ -195,8 +214,9 @@
     share = seqs // tensor_count
     swap = [(i, i ^ 1) for i in range(tensor_count)]
     own = project(
-        activations.reshape(seqs * length, width), out_grads.reshape(seqs * length, width), proj_in, proj_out
-    )
+        activations.reshape(seqs * length, width), out_grads.reshape(seqs * length, width), proj_in.T, proj_out.T
+    )
+    domains = domains.T
     other = lax.ppermute(own, "tensor", swap)
     other_queries = lax.ppermute(queries, "tensor", swap)
     sent = spread(domains, own, other, share, peers, tensor_count)

time: 44.1 us -> 35.2 us (0.80)
  Pallas kernels: 10.4 us -> 4.91 us
  local copies, waits for them, and re-layouts: 6.41 us -> 4.45 us
  blocking collectives: 25.5 us -> 23.6 us
  waiting for transfers between devices: 0.85 us -> 1.32 us
    pallas_call x1, Pallas kernels: 3.22 us -> 0.68 us  [score(): pl.pallas_call(score_kernel, out_shape=jax.ShapeDtypeStruct((peers * slot...]
    unnamed x9 -> x12, local copies, waits for them, and re-layouts: 6.41 us -> 4.45 us
    pallas_call x1, Pallas kernels: 3.74 us -> 2.1 us  [project(): pl.pallas_call(project_kernel, out_shape=jax.ShapeDtypeStruct((rows, 2 *...]
    all_to_all x1, blocking collectives: 10.9 us -> 9.38 us  [body(): lax.all_to_all(scores, ('dp', 'tensor'), split_axis=0, concat_axis=0, til...]
    pallas_call x1, Pallas kernels: 2.03 us -> 0.95 us  [spread(): pl.pallas_call(functools.partial(feature_kernel, share), out_shape=jax.Sh...]
    ppermute x1, waiting for transfers between devices: 0.84 us -> 1.31 us  [body(): other = lax.ppermute(own, 'tensor', swap)]
  transfers between devices with their start and end apart: 2 -> 2, of which waited for: 1 -> 1; matrix products, arithmetic and copies ran while one was open for 11% -> 0% of each run, Pallas kernels for 13% -> 9%
where the time goes in v2:
time: 35.2 us; the launch traced here: 34.9 us
  blocking collectives  23.6 us (67%)
  Pallas kernels  4.91 us (14%)
  local copies, waits for them, and re-layouts  4.45 us (13%)
  waiting for transfers between devices  1.32 us (4%)
  starting transfers between devices  0.58 us (2%)
    all_to_all x1, blocking collectives, body(): came = lax.all_to_all(sent, 'dp', split_axis=0, concat_axis=0, tiled=True)  14.2 us
    all_to_all x1, blocking collectives, body(): lax.all_to_all(scores, ('dp', 'tensor'), split_axis=0, concat_axis=0, til...  9.38 us
    unnamed x12, local copies, waits for them, and re-layouts  4.45 us
    pallas_call x1, Pallas kernels, project(): pl.pallas_call(project_kernel, out_shape=jax.ShapeDtypeStruct((rows, 2 *...  2.1 us
    ppermute x1, waiting for transfers between devices, body(): other = lax.ppermute(own, 'tensor', swap)  1.31 us
    pallas_call x1, Pallas kernels, pick(): pl.pallas_call(pick_kernel, out_shape=jax.ShapeDtypeStruct((share, domain...  1.19 us
    pallas_call x1, Pallas kernels, spread(): pl.pallas_call(functools.partial(feature_kernel, share), out_shape=jax.Sh...  0.95 us
  transfers between devices with their start and end apart: 2, of which 1 were waited for; matrix products, arithmetic and copies ran while one was open for 0% of the time, Pallas kernels for 9%

profile of v2, /device:TPU:0, one launch (start us, length us, event | category | flops | bytes accessed | tf_op | source)
XLA Modules:
  0.0 34.9 jit_solution(3052761301356384242)
XLA Ops:
  0.0 0.0 copy-start.5
  0.0 0.5 %collective-permute-start.1 = (bf16[192,4096]{1,0:T(8,128)(2,1)}, bf16[192,4096]{1,0:T(8,128)(2,1)S(1)}, u32[]{:S(2)}, u32[]{:S(2)}) collective-permute-start(bf16[192,4096]{1,0:T(8,128)(2,1)} %own.1), channel_id=1, source_target_pairs={{0,1},{1,0},{2,3},{3,2},{4,5},{5,4},{6,7},{7,6},{8,9},{9,8},{10,11... | collective-permute-start | bytes 4718600 | tf_op jit(solution)/shard_map/ppermute | solution.py:221
  0.5 0.0 copy-start.1
  0.5 1.3 %copy-done.1 = bf16[6,48,2048]{2,1,0:T(8,128)(2,1)S(1)} copy-done((bf16[6,48,2048]{2,1,0:T(8,128)(2,1)S(1)}, bf16[6,48,2048]{2,1,0:T(8,128)(2,1)}, u32[]{:S(2)}) %copy-start.1) | copy-done | bytes 1179672
  1.7 0.0 copy-start.2
  1.7 1.3 %copy-done.2 = bf16[6,48,2048]{2,1,0:T(8,128)(2,1)S(1)} copy-done((bf16[6,48,2048]{2,1,0:T(8,128)(2,1)S(1)}, bf16[6,48,2048]{2,1,0:T(8,128)(2,1)}, u32[]{:S(2)}) %copy-start.2) | copy-done | bytes 1179672
  3.0 0.0 copy-start.3
  3.0 0.9 %copy-done.3 = bf16[2048,64]{0,1:T(8,128)(2,1)S(1)} copy-done((bf16[2048,64]{0,1:T(8,128)(2,1)S(1)}, bf16[2048,64]{0,1:T(8,128)(2,1)}, u32[]{:S(2)}) %copy-start.3) | copy-done | bytes 262168
  3.9 0.0 copy-start.4
  4.0 0.9 %copy-done.4 = bf16[2048,64]{0,1:T(8,128)(2,1)S(1)} copy-done((bf16[2048,64]{0,1:T(8,128)(2,1)S(1)}, bf16[2048,64]{0,1:T(8,128)(2,1)}, u32[]{:S(2)}) %copy-start.4) | copy-done | bytes 262168
  4.9 0.0 copy-start
  4.9 2.1 %project.1.own = f32[288,128]{1,0:T(8,128)S(1)} custom-call(bf16[288,2048]{1,0:T(8,128)(2,1)S(1)} %bitcast.5, bf16[288,2048]{1,0:T(8,128)(2,1)S(1)} %bitcast.6, bf16[64,2048]{1,0:T(8,128)(2,1)S(1)} %bitcast.7, bf16[64,2048]{1,0:T(8,128)(2,1)S(1)} %bitcast.8), custom_call_target="tpu_custom_call" | custom-call | tf_op jit(solution)/shard_map/project/pallas_call | solution.py:66
  7.0 0.1 collective-permute-start
  7.1 1.3 %collective-permute-done.other = f32[288,128]{1,0:T(8,128)S(1)} collective-permute-done((f32[288,128]{1,0:T(8,128)S(1)}, f32[288,128]{1,0:T(8,128)S(1)}, u32[]{:S(2)}, u32[]{:S(2)}) %collective-permute-start) | collective-permute-done | bytes 147488 | tf_op jit(solution)/shard_map/ppermute | solution.py:220
  8.4 0.0 copy-done.5
  8.4 0.9 %spread.1 = bf16[8,4,16,128]{3,2,1,0:T(8,128)(2,1)S(1)} custom-call(s32[2,6]{1,0:T(2,128)S(1)} %bitcast.9, f32[288,128]{1,0:T(8,128)S(1)} %project.1.own, f32[288,128]{1,0:T(8,128)S(1)} %collective-permute-done.other), custom_call_target="tpu_custom_call" | custom-call | tf_op jit(solution)/shard_map/spread/pallas_call | solution.py:134
  9.4 14.2 %all_to_all.10.features = bf16[8,4,16,128]{3,2,1,0:T(8,128)(2,1)S(1)} all-to-all(bf16[8,4,16,128]{3,2,1,0:T(8,128)(2,1)S(1)} %spread.1), channel_id=1, replica_groups=mesh['groups'=2,'dp'=8,'tensor'=2] {'dp'}, dimensions={0} | all-to-all | bytes 262144 | tf_op jit(solution)/shard_map/all_to_all | solution.py:223
  23.6 0.0 collective-permute-done.1.other
  23.6 0.0 copy-done
  23.6 0.7 %score.1 = f32[16,2,384]{2,1,0:T(2,128)S(1)} custom-call(bf16[8,4,16,128]{3,2,1,0:T(8,128)(2,1)S(1)} %all_to_all.10.features, bf16[192,4096]{1,0:T(8,128)(2,1)S(1)} %copy-done, bf16[192,4096]{1,0:T(8,128)(2,1)S(1)} %collective-permute-done.1.other), custom_call_target="tpu_custom_call" | custom-call | tf_op jit(solution)/shard_map/score/pallas_call | solution.py:167
  24.3 9.4 %all_to_all.11.scores = f32[16,2,384]{2,1,0:T(2,128)S(1)} all-to-all(f32[16,2,384]{2,1,0:T(2,128)S(1)} %score.1), channel_id=1, replica_groups=mesh['groups'=2,'dp'=8,'tensor'=2] {'dp','tensor'}, dimensions={0} | all-to-all | bytes 98304 | tf_op jit(solution)/shard_map/all_to_all | solution.py:225
  33.7 1.2 %pick.1 = f32[3,2,384]{2,1,0:T(2,128)} custom-call(s32[2,6]{1,0:T(2,128)S(1)} %bitcast.10, f32[16,2,384]{2,1,0:T(2,128)S(1)} %all_to_all.11.scores), custom_call_target="tpu_custom_call" | custom-call | tf_op jit(solution)/shard_map/pick/pallas_call | solution.py:200
Async XLA Ops:
  0.0 8.4 %copy-start.5 = (s32[6,2]{0,1:T(2,128)S(1)}, s32[6,2]{0,1:T(2,128)}, u32[]{:S(2)}) copy-start(s32[6,2]{0,1:T(2,128)} %param.11) | copy-start | bytes 148
  0.0 23.6 %collective-permute-start.1 = (bf16[192,4096]{1,0:T(8,128)(2,1)}, bf16[192,4096]{1,0:T(8,128)(2,1)S(1)}, u32[]{:S(2)}, u32[]{:S(2)}) collective-permute-start(bf16[192,4096]{1,0:T(8,128)(2,1)} %own.1), channel_id=1, source_target_pairs={{0,1},{1,0},{2,3},{3,2},{4,5},{5,4},{6,7},{7,6},{8,9},{9,8},{10,11... | collective-permute-start | bytes 4718600 | tf_op jit(solution)/shard_map/ppermute | solution.py:221
  0.5 1.3 %copy-start.1 = (bf16[6,48,2048]{2,1,0:T(8,128)(2,1)S(1)}, bf16[6,48,2048]{2,1,0:T(8,128)(2,1)}, u32[]{:S(2)}) copy-start(bf16[6,48,2048]{2,1,0:T(8,128)(2,1)} %param.6) | copy-start | bytes 3538948
  1.7 1.3 %copy-start.2 = (bf16[6,48,2048]{2,1,0:T(8,128)(2,1)S(1)}, bf16[6,48,2048]{2,1,0:T(8,128)(2,1)}, u32[]{:S(2)}) copy-start(bf16[6,48,2048]{2,1,0:T(8,128)(2,1)} %param.7) | copy-start | bytes 3538948
  3.0 0.9 %copy-start.3 = (bf16[2048,64]{0,1:T(8,128)(2,1)S(1)}, bf16[2048,64]{0,1:T(8,128)(2,1)}, u32[]{:S(2)}) copy-start(bf16[2048,64]{0,1:T(8,128)(2,1)} %param.8) | copy-start | bytes 786436
  3.9 0.9 %copy-start.4 = (bf16[2048,64]{0,1:T(8,128)(2,1)S(1)}, bf16[2048,64]{0,1:T(8,128)(2,1)}, u32[]{:S(2)}) copy-start(bf16[2048,64]{0,1:T(8,128)(2,1)} %param.9) | copy-start | bytes 786436
  4.9 18.7 %copy-start = (bf16[192,4096]{1,0:T(8,128)(2,1)S(1)}, bf16[192,4096]{1,0:T(8,128)(2,1)}, u32[]{:S(2)}) copy-start(bf16[192,4096]{1,0:T(8,128)(2,1)} %own.1) | copy-start | bytes 4718596
  7.0 1.4 %collective-permute-start = (f32[288,128]{1,0:T(8,128)S(1)}, f32[288,128]{1,0:T(8,128)S(1)}, u32[]{:S(2)}, u32[]{:S(2)}) collective-permute-start(f32[288,128]{1,0:T(8,128)S(1)} %project.1.own), channel_id=1, source_target_pairs={{0,1},{1,0},{2,3},{3,2},{4,5},{5,4},{6,7},{7,6},{8,9},{9,8},{10,11... | collective-permute-start | bytes 442376 | tf_op jit(solution)/shard_map/ppermute | solution.py:220

commit v3 on v2

--- a/solution.py
+++ b/solution.py
@@ -24,6 +24,14 @@
             step(at)
     else:
         lax.fori_loop(0, count, lambda at, _: (step(at), 0)[1], 0)
+
+
+def near(*arrays):
+    return [pltpu.with_memory_space_constraint(x, pltpu.VMEM) for x in arrays]
+
+
+def far(*arrays):
+    return [pltpu.with_memory_space_constraint(x, pltpu.HBM) for x in arrays]
 
 
 def room(*shapes):
@@ -77,7 +85,7 @@
         ],
         compiler_params=room((acts.shape, bf16), (p_in.shape, bf16), ((rows, 2 * LANES), jnp.float32)),
         name="project",
-    )(acts, grads, p_in, p_out)
+    )(*far(acts, grads, p_in, p_out))
 
 
 def rank(domains, row, first, named):
@@ -141,7 +149,7 @@
             ((4 * own.shape[0], LANES), jnp.float32), ((peers, seqs // share * CAP, half, LANES), jnp.bfloat16)
         ),
         name="spread",
-    )(domains, own, other)
+    )(domains, *near(own, other))
 
 
 def score_kernel(features, own, other, out, rows_v):
@@ -177,7 +185,7 @@
             ((peers * slots // CAP, 8, 2 * own.shape[0]), jnp.float32),
         ),
         name="score",
-    )(features, own, other)
+    )(*near(features, own, other))
 
 
 def pick_kernel(domains, scores, out):
@@ -204,7 +212,7 @@
         out_specs=VMEM,
         compiler_params=room((scores.shape, jnp.float32), ((8 * share, domains.shape[0], scores.shape[2]), jnp.float32)),
         name="pick",
-    )(domains, scores)
+    )(domains, *near(scores))
 
 
 def body(activations, out_grads, proj_in, proj_out, queries, domains):

time: 35.2 us -> 31.6 us (0.90)
  local copies, waits for them, and re-layouts: 4.45 us -> 0.01 us
  Pallas kernels: 4.91 us -> 5.84 us
    unnamed x12 -> x4, local copies, waits for them, and re-layouts: 4.45 us -> 0.01 us
    pallas_call x1, Pallas kernels: 2.1 us -> 3.03 us  [project(): pl.pallas_call(project_kernel, out_shape=jax.ShapeDtypeStruct((rows, 2 *...]
  transfers between devices with their start and end apart: 2 -> 2, of which waited for: 1 -> 1; matrix products, arithmetic and copies ran while one was open for 0% -> 0% of each run, Pallas kernels for 9% -> 13%
where the time goes in v3:
time: 31.6 us; the launch traced here: 31.4 us
  blocking collectives  23.6 us (75%)
  Pallas kernels  5.84 us (18%)
  waiting for transfers between devices  1.32 us (4%)
  starting transfers between devices  0.57 us (2%)
    all_to_all x1, blocking collectives, body(): came = lax.all_to_all(sent, 'dp', split_axis=0, concat_axis=0, tiled=True)  14.2 us
    all_to_all x1, blocking collectives, body(): lax.all_to_all(scores, ('dp', 'tensor'), split_axis=0, concat_axis=0, til...  9.38 us
    pallas_call x1, Pallas kernels, project(): pl.pallas_call(project_kernel, out_shape=jax.ShapeDtypeStruct((rows, 2 *...  3.03 us
    ppermute x1, waiting for transfers between devices, body(): other = lax.ppermute(own, 'tensor', swap)  1.32 us
    pallas_call x1, Pallas kernels, pick(): pl.pallas_call(pick_kernel, out_shape=jax.ShapeDtypeStruct((share, domain...  1.19 us
    pallas_call x1, Pallas kernels, spread(): pl.pallas_call(functools.partial(feature_kernel, share), out_shape=jax.Sh...  0.95 us
    pallas_call x1, Pallas kernels, score(): pl.pallas_call(score_kernel, out_shape=jax.ShapeDtypeStruct((peers * slot...  0.68 us
  transfers between devices with their start and end apart: 2, of which 1 were waited for; matrix products, arithmetic and copies ran while one was open for 0% of the time, Pallas kernels for 13%

profile of v3, /device:TPU:0, one launch (start us, length us, event | category | flops | bytes accessed | tf_op | source)
XLA Modules:
  0.0 31.4 jit_solution(13880658203711485048)
XLA Ops:
  0.0 0.0 copy-start.1
  0.0 0.5 %collective-permute-start.1 = (bf16[192,4096]{1,0:T(8,128)(2,1)}, bf16[192,4096]{1,0:T(8,128)(2,1)S(1)}, u32[]{:S(2)}, u32[]{:S(2)}) collective-permute-start(bf16[192,4096]{1,0:T(8,128)(2,1)} %own.1), channel_id=1, source_target_pairs={{0,1},{1,0},{2,3},{3,2},{4,5},{5,4},{6,7},{7,6},{8,9},{9,8},{10,11... | collective-permute-start | bytes 4718600 | tf_op jit(solution)/shard_map/ppermute | solution.py:229
  0.5 0.0 copy-start
  0.5 3.0 %project.1.own = f32[288,128]{1,0:T(8,128)S(1)} custom-call(bf16[288,2048]{1,0:T(8,128)(2,1)} %bitcast.7, bf16[288,2048]{1,0:T(8,128)(2,1)} %bitcast.8, bf16[64,2048]{1,0:T(8,128)(2,1)} %bitcast.9, bf16[64,2048]{1,0:T(8,128)(2,1)} %bitcast.10), custom_call_target="tpu_custom_call" | custom-call | tf_op jit(solution)/shard_map/project/pallas_call | solution.py:74
  3.5 0.1 collective-permute-start
  3.6 1.3 %collective-permute-done.other = f32[288,128]{1,0:T(8,128)S(1)} collective-permute-done((f32[288,128]{1,0:T(8,128)S(1)}, f32[288,128]{1,0:T(8,128)S(1)}, u32[]{:S(2)}, u32[]{:S(2)}) %collective-permute-start) | collective-permute-done | bytes 147488 | tf_op jit(solution)/shard_map/ppermute | solution.py:228
  4.9 0.0 copy-done.1
  4.9 0.9 %spread.1 = bf16[8,4,16,128]{3,2,1,0:T(8,128)(2,1)S(1)} custom-call(s32[2,6]{1,0:T(2,128)S(1)} %bitcast.5, f32[288,128]{1,0:T(8,128)S(1)} %project.1.own, f32[288,128]{1,0:T(8,128)S(1)} %collective-permute-done.other), custom_call_target="tpu_custom_call" | custom-call | tf_op jit(solution)/shard_map/spread/pallas_call | solution.py:142
  5.9 14.2 %all_to_all.10.features = bf16[8,4,16,128]{3,2,1,0:T(8,128)(2,1)S(1)} all-to-all(bf16[8,4,16,128]{3,2,1,0:T(8,128)(2,1)S(1)} %spread.1), channel_id=1, replica_groups=mesh['groups'=2,'dp'=8,'tensor'=2] {'dp'}, dimensions={0} | all-to-all | bytes 262144 | tf_op jit(solution)/shard_map/all_to_all | solution.py:231
  20.1 0.0 collective-permute-done.1.other
  20.1 0.0 copy-done
  20.1 0.7 %score.1 = f32[16,2,384]{2,1,0:T(2,128)S(1)} custom-call(bf16[8,4,16,128]{3,2,1,0:T(8,128)(2,1)S(1)} %all_to_all.10.features, bf16[192,4096]{1,0:T(8,128)(2,1)S(1)} %copy-done, bf16[192,4096]{1,0:T(8,128)(2,1)S(1)} %collective-permute-done.1.other), custom_call_target="tpu_custom_call" | custom-call | tf_op jit(solution)/shard_map/score/pallas_call | solution.py:175
  20.8 9.4 %all_to_all.11.scores = f32[16,2,384]{2,1,0:T(2,128)S(1)} all-to-all(f32[16,2,384]{2,1,0:T(2,128)S(1)} %score.1), channel_id=1, replica_groups=mesh['groups'=2,'dp'=8,'tensor'=2] {'dp','tensor'}, dimensions={0} | all-to-all | bytes 98304 | tf_op jit(solution)/shard_map/all_to_all | solution.py:233
  30.2 1.2 %pick.1 = f32[3,2,384]{2,1,0:T(2,128)} custom-call(s32[2,6]{1,0:T(2,128)S(1)} %bitcast.6, f32[16,2,384]{2,1,0:T(2,128)S(1)} %all_to_all.11.scores), custom_call_target="tpu_custom_call" | custom-call | tf_op jit(solution)/shard_map/pick/pallas_call | solution.py:208
Async XLA Ops:
  0.0 4.9 %copy-start.1 = (s32[6,2]{0,1:T(2,128)S(1)}, s32[6,2]{0,1:T(2,128)}, u32[]{:S(2)}) copy-start(s32[6,2]{0,1:T(2,128)} %param.11) | copy-start | bytes 148
  0.0 20.1 %collective-permute-start.1 = (bf16[192,4096]{1,0:T(8,128)(2,1)}, bf16[192,4096]{1,0:T(8,128)(2,1)S(1)}, u32[]{:S(2)}, u32[]{:S(2)}) collective-permute-start(bf16[192,4096]{1,0:T(8,128)(2,1)} %own.1), channel_id=1, source_target_pairs={{0,1},{1,0},{2,3},{3,2},{4,5},{5,4},{6,7},{7,6},{8,9},{9,8},{10,11... | collective-permute-start | bytes 4718600 | tf_op jit(solution)/shard_map/ppermute | solution.py:229
  0.5 19.7 %copy-start = (bf16[192,4096]{1,0:T(8,128)(2,1)S(1)}, bf16[192,4096]{1,0:T(8,128)(2,1)}, u32[]{:S(2)}) copy-start(bf16[192,4096]{1,0:T(8,128)(2,1)} %own.1) | copy-start | bytes 4718596
  3.5 1.4 %collective-permute-start = (f32[288,128]{1,0:T(8,128)S(1)}, f32[288,128]{1,0:T(8,128)S(1)}, u32[]{:S(2)}, u32[]{:S(2)}) collective-permute-start(f32[288,128]{1,0:T(8,128)S(1)} %project.1.own), channel_id=1, source_target_pairs={{0,1},{1,0},{2,3},{3,2},{4,5},{5,4},{6,7},{7,6},{8,9},{9,8},{10,11... | collective-permute-start | bytes 442376 | tf_op jit(solution)/shard_map/ppermute | solution.py:228

commit v4 on v3

--- a/solution.py
+++ b/solution.py
@@ -102,7 +102,9 @@
     return found
 
 
-def feature_kernel(share, domains, own, other, out, grams):
+def feature_kernel(share, domains_in, own, other, out, grams, domains, sem):
+    fetch = pltpu.make_async_copy(domains_in, domains, sem)
+    fetch.start()
     fanout, seqs = domains.shape
     length = own.shape[0] // seqs
     proj = own.shape[1] // 2
@@ -122,6 +124,7 @@
             (((0,), (0,)), ((), ())),
             preferred_element_type=jnp.float32,
         )
+    fetch.wait()
     for s in range(seqs):
         even = grams[s, pl.ds(mine, half, stride=2), :]
         odd = grams[s, pl.ds(mine + 1, half, stride=2), :]
@@ -142,9 +145,13 @@
     return pl.pallas_call(
         functools.partial(feature_kernel, share),
         out_shape=jax.ShapeDtypeStruct((peers, seqs // share * CAP, half, LANES), jnp.bfloat16),
-        in_specs=[SMEM, VMEM, VMEM],
-        out_specs=VMEM,
-        scratch_shapes=[pltpu.VMEM((seqs, 2 * proj, 2 * proj), jnp.float32)],
+        in_specs=[ANY, VMEM, VMEM],
+        out_specs=VMEM,
+        scratch_shapes=[
+            pltpu.VMEM((seqs, 2 * proj, 2 * proj), jnp.float32),
+            pltpu.SMEM(domains.shape, jnp.int32),
+            pltpu.SemaphoreType.DMA,
+        ],
         compiler_params=room(
             ((4 * own.shape[0], LANES), jnp.float32), ((peers, seqs // share * CAP, half, LANES), jnp.bfloat16)
         ),
@@ -188,31 +195,54 @@
     )(*near(features, own, other))
 
 
-def pick_kernel(domains, scores, out):
-    share, fanout, _ = out.shape
+def plan_kernel(share, domains, own, out):
+    del own
+    fanout = domains.shape[0]
     first = lax.axis_index("tensor") * share
+    column = lax.broadcasted_iota(jnp.int32, (1, out.shape[1]), 1)
+    out[...] = jnp.zeros_like(out)
     for s in range(share):
 
-        def take(k, s=s):
+        def mark(k, s=s):
             named = domains[k, first + s]
             found = jnp.int32(0)
             for other in range(s):
                 found += sum((domains[j, first + other] == named).astype(jnp.int32) for j in range(fanout))
-            both = scores[2 * named] + scores[2 * named + 1]
-            out[s, pl.ds(k, 1)] = jnp.where(found == 0, both[0:1], both[1:2])
-
-        each(fanout, take)
-
-
-def pick(domains, scores, share):
+            row = 2 * CAP * named + found
+            out[pl.ds(s * fanout + k, 1)] = ((column == row) | (column == row + CAP)).astype(jnp.float32)
+
+        each(fanout, mark)
+
+
+def plan(domains, own, share, count):
+    rows = -(-share * domains.shape[0] // 8) * 8
+    return pl.pallas_call(
+        functools.partial(plan_kernel, share),
+        out_shape=jax.ShapeDtypeStruct((rows, count), jnp.float32),
+        in_specs=[SMEM, ANY],
+        out_specs=VMEM,
+        compiler_params=room(((rows, max(count, LANES)), jnp.float32)),
+        name="plan",
+    )(domains, own)
+
+
+def pick_kernel(chosen, scores, out):
+    share, fanout, _ = out.shape
+    rows = jnp.concatenate([scores[p] for p in range(scores.shape[0])], axis=0)
+    picked = jnp.dot(chosen[...], rows, precision=lax.Precision.HIGHEST, preferred_element_type=jnp.float32)
+    for s in range(share):
+        out[s] = picked[s * fanout : (s + 1) * fanout]
+
+
+def pick(chosen, scores, share, fanout):
     return pl.pallas_call(
         pick_kernel,
-        out_shape=jax.ShapeDtypeStruct((share, domains.shape[0], scores.shape[2]), jnp.float32),
-        in_specs=[SMEM, VMEM],
-        out_specs=VMEM,
-        compiler_params=room((scores.shape, jnp.float32), ((8 * share, domains.shape[0], scores.shape[2]), jnp.float32)),
+        out_shape=jax.ShapeDtypeStruct((share, fanout, scores.shape[2]), jnp.float32),
+        in_specs=[VMEM, VMEM],
+        out_specs=VMEM,
+        compiler_params=room((scores.shape, jnp.float32), (scores.shape, jnp.float32), (chosen.shape, jnp.float32)),
         name="pick",
-    )(domains, *near(scores))
+    )(*near(chosen, scores))
 
 
 def body(activations, out_grads, proj_in, proj_out, queries, domains):
@@ -226,12 +256,14 @@
     )
     domains = domains.T
     other = lax.ppermute(own, "tensor", swap)
+    chosen = plan(domains, own, share, peers * tensor_count * CAP)
+    queries, other, chosen = lax.optimization_barrier((queries, other, chosen))
     other_queries = lax.ppermute(queries, "tensor", swap)
     sent = spread(domains, own, other, share, peers, tensor_count)
     came = lax.all_to_all(sent, "dp", split_axis=0, concat_axis=0, tiled=True)
     scores = score(came, queries, other_queries)
     back = lax.all_to_all(scores, ("dp", "tensor"), split_axis=0, concat_axis=0, tiled=True)
-    return pick(domains, back, share)
+    return pick(chosen, back, share, domains.shape[0])
 
 
 def solution(mesh):

time: 31.6 us -> 30.9 us (0.978)
  waiting for transfers between devices: 1.32 us -> 0.41 us
    ppermute x1, waiting for transfers between devices: 1.32 us -> 0.41 us  [body(): other = lax.ppermute(own, 'tensor', swap)]
    ppermute x1, starting transfers between devices: 0.12 us -> 0.52 us  [body(): other = lax.ppermute(own, 'tensor', swap)]
    pallas_call x1 -> x2, Pallas kernels: 1.19 us -> 1.36 us  [the longest x1 0.77 us: pick(): pl.pallas_call(pick_kernel, out_shape=jax.ShapeDtypeStruct((share, fanout...]
  transfers between devices with their start and end apart: 2 -> 2, of which waited for: 1 -> 1; matrix products, arithmetic and copies ran while one was open for 0% -> 0% of each run, Pallas kernels for 13% -> 4%
where the time goes in v4:
time: 30.9 us; the launch traced here: 30.7 us
  blocking collectives  23.6 us (76%)
  Pallas kernels  5.7 us (18%)
  starting transfers between devices  0.88 us (3%)
  waiting for transfers between devices  0.41 us (1%)
    all_to_all x1, blocking collectives, body(): came = lax.all_to_all(sent, 'dp', split_axis=0, concat_axis=0, tiled=True)  14.3 us
    all_to_all x1, blocking collectives, body(): lax.all_to_all(scores, ('dp', 'tensor'), split_axis=0, concat_axis=0, til...  9.38 us
    pallas_call x1, Pallas kernels, project(): pl.pallas_call(project_kernel, out_shape=jax.ShapeDtypeStruct((rows, 2 *...  3.02 us
    pallas_call x1, Pallas kernels, pick(): pl.pallas_call(pick_kernel, out_shape=jax.ShapeDtypeStruct((share, fanout...  0.77 us
    pallas_call x1, Pallas kernels, score(): pl.pallas_call(score_kernel, out_shape=jax.ShapeDtypeStruct((peers * slot...  0.68 us
    pallas_call x1, Pallas kernels, spread(): pl.pallas_call(functools.partial(feature_kernel, share), out_shape=jax.Sh...  0.64 us
  transfers between devices with their start and end apart: 2, of which 1 were waited for; matrix products, arithmetic and copies ran while one was open for 0% of the time, Pallas kernels for 4%

profile of v4, /device:TPU:0, one launch (start us, length us, event | category | flops | bytes accessed | tf_op | source)
XLA Modules:
  0.0 30.7 jit_solution(10776296620013347461)
XLA Ops:
  0.0 0.0 copy-start.1
  0.0 0.0 copy-start
  0.0 3.0 %project.1.own = f32[288,128]{1,0:T(8,128)S(1)} custom-call(bf16[288,2048]{1,0:T(8,128)(2,1)} %bitcast.7, bf16[288,2048]{1,0:T(8,128)(2,1)} %bitcast.8, bf16[64,2048]{1,0:T(8,128)(2,1)} %bitcast.9, bf16[64,2048]{1,0:T(8,128)(2,1)} %bitcast.10), custom_call_target="tpu_custom_call" | custom-call | tf_op jit(solution)/shard_map/project/pallas_call | solution.py:74
  3.0 0.5 %collective-permute-start = (f32[288,128]{1,0:T(8,128)S(1)}, f32[288,128]{1,0:T(8,128)S(1)}, u32[]{:S(2)}, u32[]{:S(2)}) collective-permute-start(f32[288,128]{1,0:T(8,128)S(1)} %project.1.own), channel_id=1, source_target_pairs={{0,1},{1,0},{2,3},{3,2},{4,5},{5,4},{6,7},{7,6},{8,9},{9,8},{10,11... | collective-permute-start | bytes 442376 | tf_op jit(solution)/shard_map/ppermute | solution.py:258
  3.6 0.0 copy-done.1
  3.6 0.6 %plan.1.chosen = f32[8,32]{1,0:T(8,128)S(1)} custom-call(s32[2,6]{1,0:T(2,128)S(1)} %bitcast.5, f32[288,128]{1,0:T(8,128)S(1)} %project.1.own), custom_call_target="tpu_custom_call" | custom-call | tf_op jit(solution)/shard_map/plan/pallas_call | solution.py:219
  4.2 0.4 %collective-permute-done.other = f32[288,128]{1,0:T(8,128)S(1)} collective-permute-done((f32[288,128]{1,0:T(8,128)S(1)}, f32[288,128]{1,0:T(8,128)S(1)}, u32[]{:S(2)}, u32[]{:S(2)}) %collective-permute-start) | collective-permute-done | bytes 147488 | tf_op jit(solution)/shard_map/ppermute | solution.py:258
  4.6 0.0 copy-done
  4.6 0.4 %collective-permute-start.1 = (bf16[192,4096]{1,0:T(8,128)(2,1)S(1)}, bf16[192,4096]{1,0:T(8,128)(2,1)S(1)}, u32[]{:S(2)}, u32[]{:S(2)}) collective-permute-start(bf16[192,4096]{1,0:T(8,128)(2,1)S(1)} %copy-done), channel_id=1, source_target_pairs={{0,1},{1,0},{2,3},{3,2},{4,5},{5,4},{6,7},{7,6},{8,9},{9,8},{10,11... | collective-permute-start | bytes 4718600 | tf_op jit(solution)/shard_map/ppermute | solution.py:261
  4.9 0.6 %spread.1 = bf16[8,4,16,128]{3,2,1,0:T(8,128)(2,1)S(1)} custom-call(s32[2,6]{1,0:T(2,128)S(1)} %bitcast.6, f32[288,128]{1,0:T(8,128)S(1)} %project.1.own, f32[288,128]{1,0:T(8,128)S(1)} %collective-permute-done.other), custom_call_target="tpu_custom_call" | custom-call | tf_op jit(solution)/shard_map/spread/pallas_call | solution.py:145
  5.6 14.3 %all_to_all.10.features = bf16[8,4,16,128]{3,2,1,0:T(8,128)(2,1)S(1)} all-to-all(bf16[8,4,16,128]{3,2,1,0:T(8,128)(2,1)S(1)} %spread.1), channel_id=1, replica_groups=mesh['groups'=2,'dp'=8,'tensor'=2] {'dp'}, dimensions={0} | all-to-all | bytes 262144 | tf_op jit(solution)/shard_map/all_to_all | solution.py:263
  19.8 0.0 collective-permute-done.1.other
  19.8 0.7 %score.1 = f32[16,2,384]{2,1,0:T(2,128)S(1)} custom-call(bf16[8,4,16,128]{3,2,1,0:T(8,128)(2,1)S(1)} %all_to_all.10.features, bf16[192,4096]{1,0:T(8,128)(2,1)S(1)} %copy-done, bf16[192,4096]{1,0:T(8,128)(2,1)S(1)} %collective-permute-done.1.other), custom_call_target="tpu_custom_call" | custom-call | tf_op jit(solution)/shard_map/score/pallas_call | solution.py:182
  20.5 9.4 %all_to_all.11.scores = f32[16,2,384]{2,1,0:T(2,128)S(1)} all-to-all(f32[16,2,384]{2,1,0:T(2,128)S(1)} %score.1), channel_id=1, replica_groups=mesh['groups'=2,'dp'=8,'tensor'=2] {'dp','tensor'}, dimensions={0} | all-to-all | bytes 98304 | tf_op jit(solution)/shard_map/all_to_all | solution.py:265
  29.9 0.8 %pick.1 = f32[3,2,384]{2,1,0:T(2,128)} custom-call(f32[8,32]{1,0:T(8,128)S(1)} %plan.1.chosen, f32[16,2,384]{2,1,0:T(2,128)S(1)} %all_to_all.11.scores), custom_call_target="tpu_custom_call" | custom-call | tf_op jit(solution)/shard_map/pick/pallas_call | solution.py:238
Async XLA Ops:
  0.0 3.6 %copy-start.1 = (s32[6,2]{0,1:T(2,128)S(1)}, s32[6,2]{0,1:T(2,128)}, u32[]{:S(2)}) copy-start(s32[6,2]{0,1:T(2,128)} %param.11) | copy-start | bytes 148
  0.0 4.6 %copy-start = (bf16[192,4096]{1,0:T(8,128)(2,1)S(1)}, bf16[192,4096]{1,0:T(8,128)(2,1)}, u32[]{:S(2)}) copy-start(bf16[192,4096]{1,0:T(8,128)(2,1)} %own) | copy-start | bytes 4718596
  3.0 1.5 %collective-permute-start = (f32[288,128]{1,0:T(8,128)S(1)}, f32[288,128]{1,0:T(8,128)S(1)}, u32[]{:S(2)}, u32[]{:S(2)}) collective-permute-start(f32[288,128]{1,0:T(8,128)S(1)} %project.1.own), channel_id=1, source_target_pairs={{0,1},{1,0},{2,3},{3,2},{4,5},{5,4},{6,7},{7,6},{8,9},{9,8},{10,11... | collective-permute-start | bytes 442376 | tf_op jit(solution)/shard_map/ppermute | solution.py:258
  4.6 15.3 %collective-permute-start.1 = (bf16[192,4096]{1,0:T(8,128)(2,1)S(1)}, bf16[192,4096]{1,0:T(8,128)(2,1)S(1)}, u32[]{:S(2)}, u32[]{:S(2)}) collective-permute-start(bf16[192,4096]{1,0:T(8,128)(2,1)S(1)} %copy-done), channel_id=1, source_target_pairs={{0,1},{1,0},{2,3},{3,2},{4,5},{5,4},{6,7},{7,6},{8,9},{9,8},{10,11... | collective-permute-start | bytes 4718600 | tf_op jit(solution)/shard_map/ppermute | solution.py:261

commit v5 on v4

--- a/solution.py
+++ b/solution.py
@@ -9,7 +9,6 @@
 from jax.sharding import PartitionSpec as P
 
 CAP = 2
-CHUNKS = 4
 LANES = 128
 LAST = (((1,), (1,)), ((), ()))
 
@@ -39,32 +38,18 @@
     return pltpu.CompilerParams(vmem_limit_bytes=2 * held + (1 << 20))
 
 
-def project_kernel(acts, grads, p_in, p_out, out, acts_v, grads_v, in_v, out_v, sems):
-    width = acts.shape[1]
-    size = width // CHUNKS
-    copies = []
-    for side, (x, x_v, w, w_v) in enumerate(((acts, acts_v, p_in, in_v), (grads, grads_v, p_out, out_v))):
-        for c in range(CHUNKS):
-            part = pl.ds(c * size, size)
-            copies.append(
-                (
-                    pltpu.make_async_copy(w.at[:, part], w_v.at[:, part], sems.at[side, c, 0]),
-                    pltpu.make_async_copy(x.at[:, part], x_v.at[c], sems.at[side, c, 1]),
-                )
-            )
-    for pair in copies:
-        for copy in pair:
-            copy.start()
-    sums = []
-    for side, (x_v, w_v) in enumerate(((acts_v, in_v), (grads_v, out_v))):
-        total = None
-        for c in range(CHUNKS):
-            for copy in copies[side * CHUNKS + c]:
-                copy.wait()
-            term = lax.dot_general(x_v[c], w_v[:, pl.ds(c * size, size)], LAST, preferred_element_type=jnp.float32)
-            total = term if total is None else total + term
-        sums.append(total)
-    out[...] = jnp.concatenate(sums, axis=1)
+def project_kernel(acts, grads, p_in, p_out, out, x_v, w_v, sums, sems):
+    for side, (x, w) in enumerate(((acts, p_in), (grads, p_out))):
+        pltpu.make_async_copy(w, w_v.at[side], sems.at[side, 0]).start()
+        pltpu.make_async_copy(x, x_v.at[side], sems.at[side, 1]).start()
+
+    @pl.loop(0, 2)
+    def _(side):
+        pltpu.make_async_copy(p_in, w_v.at[side], sems.at[side, 0]).wait()
+        pltpu.make_async_copy(acts, x_v.at[side], sems.at[side, 1]).wait()
+        sums[side] = lax.dot_general(x_v[side], w_v[side], LAST, preferred_element_type=jnp.float32)
+
+    out[...] = jnp.concatenate([sums[0], sums[1]], axis=1)
 
 
 def project(acts, grads, p_in, p_out):
@@ -77,13 +62,12 @@
         in_specs=[ANY] * 4,
         out_specs=VMEM,
         scratch_shapes=[
-            pltpu.VMEM((CHUNKS, rows, width // CHUNKS), jnp.bfloat16),
-            pltpu.VMEM((CHUNKS, rows, width // CHUNKS), jnp.bfloat16),
-            pltpu.VMEM((proj, width), jnp.bfloat16),
-            pltpu.VMEM((proj, width), jnp.bfloat16),
-            pltpu.SemaphoreType.DMA((2, CHUNKS, 2)),
+            pltpu.VMEM((2, rows, width), bf16),
+            pltpu.VMEM((2, proj, width), bf16),
+            pltpu.VMEM((2, rows, proj), jnp.float32),
+            pltpu.SemaphoreType.DMA((2, 2)),
         ],
-        compiler_params=room((acts.shape, bf16), (p_in.shape, bf16), ((rows, 2 * LANES), jnp.float32)),
+        compiler_params=room((acts.shape, bf16), (p_in.shape, bf16), ((rows, 4 * LANES), jnp.float32)),
         name="project",
     )(*far(acts, grads, p_in, p_out))
 
@@ -155,6 +139,7 @@
         compiler_params=room(
             ((4 * own.shape[0], LANES), jnp.float32), ((peers, seqs // share * CAP, half, LANES), jnp.bfloat16)
         ),
+        cost_estimate=pl.CostEstimate(flops=50_000_000_000, bytes_accessed=1 << 20, transcendentals=0),
         name="spread",
     )(domains, *near(own, other))
 
@@ -257,7 +242,7 @@
     domains = domains.T
     other = lax.ppermute(own, "tensor", swap)
     chosen = plan(domains, own, share, peers * tensor_count * CAP)
-    queries, other, chosen = lax.optimization_barrier((queries, other, chosen))
+    queries, chosen = lax.optimization_barrier((queries, chosen))
     other_queries = lax.ppermute(queries, "tensor", swap)
     sent = spread(domains, own, other, share, peers, tensor_count)
     came = lax.all_to_all(sent, "dp", split_axis=0, concat_axis=0, tiled=True)

time: 30.9 us -> 30 us (0.971)
  Pallas kernels: 5.7 us -> 5.19 us
    pallas_call x1, Pallas kernels: 3.02 us -> 2.52 us  [project(): pl.pallas_call(project_kernel, out_shape=jax.ShapeDtypeStruct((rows, 2 *...]
where the time goes in v5:
time: 30 us; the launch traced here: 29.8 us
  blocking collectives  23.6 us (79%)
  Pallas kernels  5.19 us (17%)
  starting transfers between devices  0.64 us (2%)
    all_to_all x1, blocking collectives, body(): came = lax.all_to_all(sent, 'dp', split_axis=0, concat_axis=0, tiled=True)  14.3 us
    all_to_all x1, blocking collectives, body(): lax.all_to_all(scores, ('dp', 'tensor'), split_axis=0, concat_axis=0, til...  9.34 us
    pallas_call x1, Pallas kernels, project(): pl.pallas_call(project_kernel, out_shape=jax.ShapeDtypeStruct((rows, 2 *...  2.52 us
    pallas_call x1, Pallas kernels, pick(): pl.pallas_call(pick_kernel, out_shape=jax.ShapeDtypeStruct((share, fanout...  0.77 us
    pallas_call x1, Pallas kernels, score(): pl.pallas_call(score_kernel, out_shape=jax.ShapeDtypeStruct((peers * slot...  0.68 us
    pallas_call x1, Pallas kernels, spread(): pl.pallas_call(functools.partial(feature_kernel, share), out_shape=jax.Sh...  0.64 us
  transfers between devices with their start and end apart: 2, of which 1 were waited for; matrix products, arithmetic and copies ran while one was open for 0% of the time, Pallas kernels for 4%

profile of v5, /device:TPU:0, one launch (start us, length us, event | category | flops | bytes accessed | tf_op | source)
XLA Modules:
  0.0 29.8 jit_solution(6407687933808287867)
XLA Ops:
  0.0 0.0 copy-start.1
  0.0 0.0 copy-start
  0.0 2.5 %project.1.own = f32[288,128]{1,0:T(8,128)S(1)} custom-call(bf16[288,2048]{1,0:T(8,128)(2,1)} %bitcast.7, bf16[288,2048]{1,0:T(8,128)(2,1)} %bitcast.8, bf16[64,2048]{1,0:T(8,128)(2,1)} %bitcast.9, bf16[64,2048]{1,0:T(8,128)(2,1)} %bitcast.10), custom_call_target="tpu_custom_call" | custom-call | tf_op jit(solution)/shard_map/project/pallas_call | solution.py:59
  2.5 0.5 %collective-permute-start = (f32[288,128]{1,0:T(8,128)S(1)}, f32[288,128]{1,0:T(8,128)S(1)}, u32[]{:S(2)}, u32[]{:S(2)}) collective-permute-start(f32[288,128]{1,0:T(8,128)S(1)} %project.1.own), channel_id=1, source_target_pairs={{0,1},{1,0},{2,3},{3,2},{4,5},{5,4},{6,7},{7,6},{8,9},{9,8},{10,11... | collective-permute-start | bytes 442376 | tf_op jit(solution)/shard_map/ppermute | solution.py:243
  3.0 0.0 copy-done.1
  3.1 0.6 %plan.1.chosen = f32[8,32]{1,0:T(8,128)S(1)} custom-call(s32[2,6]{1,0:T(2,128)S(1)} %bitcast.5, f32[288,128]{1,0:T(8,128)S(1)} %project.1.own), custom_call_target="tpu_custom_call" | custom-call | tf_op jit(solution)/shard_map/plan/pallas_call | solution.py:204
  3.6 0.0 copy-done
  3.7 0.1 collective-permute-start.1
  3.8 0.3 collective-permute-done.other
  4.1 0.6 %spread.1 = bf16[8,4,16,128]{3,2,1,0:T(8,128)(2,1)S(1)} custom-call(s32[2,6]{1,0:T(2,128)S(1)} %bitcast.6, f32[288,128]{1,0:T(8,128)S(1)} %project.1.own, f32[288,128]{1,0:T(8,128)S(1)} %collective-permute-done.other), custom_call_target="tpu_custom_call" | custom-call | flops 49999998976 | bytes 1048576 | tf_op jit(solution)/shard_map/spread/pallas_call | solution.py:129
  4.7 14.3 %all_to_all.10.features = bf16[8,4,16,128]{3,2,1,0:T(8,128)(2,1)S(1)} all-to-all(bf16[8,4,16,128]{3,2,1,0:T(8,128)(2,1)S(1)} %spread.1), channel_id=1, replica_groups=mesh['groups'=2,'dp'=8,'tensor'=2] {'dp'}, dimensions={0} | all-to-all | bytes 262144 | tf_op jit(solution)/shard_map/all_to_all | solution.py:248
  19.0 0.0 collective-permute-done.1.other
  19.0 0.7 %score.1 = f32[16,2,384]{2,1,0:T(2,128)S(1)} custom-call(bf16[8,4,16,128]{3,2,1,0:T(8,128)(2,1)S(1)} %all_to_all.10.features, bf16[192,4096]{1,0:T(8,128)(2,1)S(1)} %copy-done, bf16[192,4096]{1,0:T(8,128)(2,1)S(1)} %collective-permute-done.1.other), custom_call_target="tpu_custom_call" | custom-call | tf_op jit(solution)/shard_map/score/pallas_call | solution.py:167
  19.7 9.3 %all_to_all.11.scores = f32[16,2,384]{2,1,0:T(2,128)S(1)} all-to-all(f32[16,2,384]{2,1,0:T(2,128)S(1)} %score.1), channel_id=1, replica_groups=mesh['groups'=2,'dp'=8,'tensor'=2] {'dp','tensor'}, dimensions={0} | all-to-all | bytes 98304 | tf_op jit(solution)/shard_map/all_to_all | solution.py:250
  29.0 0.8 %pick.1 = f32[3,2,384]{2,1,0:T(2,128)} custom-call(f32[8,32]{1,0:T(8,128)S(1)} %plan.1.chosen, f32[16,2,384]{2,1,0:T(2,128)S(1)} %all_to_all.11.scores), custom_call_target="tpu_custom_call" | custom-call | tf_op jit(solution)/shard_map/pick/pallas_call | solution.py:223
Async XLA Ops:
  0.0 3.1 %copy-start.1 = (s32[6,2]{0,1:T(2,128)S(1)}, s32[6,2]{0,1:T(2,128)}, u32[]{:S(2)}) copy-start(s32[6,2]{0,1:T(2,128)} %param.11) | copy-start | bytes 148
  0.0 3.6 %copy-start = (bf16[192,4096]{1,0:T(8,128)(2,1)S(1)}, bf16[192,4096]{1,0:T(8,128)(2,1)}, u32[]{:S(2)}) copy-start(bf16[192,4096]{1,0:T(8,128)(2,1)} %own) | copy-start | bytes 4718596
  2.5 1.5 %collective-permute-start = (f32[288,128]{1,0:T(8,128)S(1)}, f32[288,128]{1,0:T(8,128)S(1)}, u32[]{:S(2)}, u32[]{:S(2)}) collective-permute-start(f32[288,128]{1,0:T(8,128)S(1)} %project.1.own), channel_id=1, source_target_pairs={{0,1},{1,0},{2,3},{3,2},{4,5},{5,4},{6,7},{7,6},{8,9},{9,8},{10,11... | collective-permute-start | bytes 442376 | tf_op jit(solution)/shard_map/ppermute | solution.py:243
  3.7 15.4 %collective-permute-start.1 = (bf16[192,4096]{1,0:T(8,128)(2,1)S(1)}, bf16[192,4096]{1,0:T(8,128)(2,1)S(1)}, u32[]{:S(2)}, u32[]{:S(2)}) collective-permute-start(bf16[192,4096]{1,0:T(8,128)(2,1)S(1)} %copy-done), channel_id=1, source_target_pairs={{0,1},{1,0},{2,3},{3,2},{4,5},{5,4},{6,7},{7,6},{8,9},{9,8},{10,11... | collective-permute-start | bytes 4718600 | tf_op jit(solution)/shard_map/ppermute | solution.py:246

commit v6 on v5

--- a/solution.py
+++ b/solution.py
@@ -39,7 +39,7 @@
 
 
 def project_kernel(acts, grads, p_in, p_out, out, x_v, w_v, sums, sems):
-    for side, (x, w) in enumerate(((acts, p_in), (grads, p_out))):
+    for side, (x, w) in enumerate(((grads, p_out), (acts, p_in))):
         pltpu.make_async_copy(w, w_v.at[side], sems.at[side, 0]).start()
         pltpu.make_async_copy(x, x_v.at[side], sems.at[side, 1]).start()
 
@@ -86,10 +86,8 @@
     return found
 
 
-def feature_kernel(share, domains_in, own, other, out, grams, domains, sem):
-    fetch = pltpu.make_async_copy(domains_in, domains, sem)
-    fetch.start()
-    fanout, seqs = domains.shape
+def feature_kernel(table, own, other, out, grams):
+    fanout, seqs = table.shape
     length = own.shape[0] // seqs
     proj = own.shape[1] // 2
     half = out.shape[2]
@@ -97,51 +95,45 @@
     both = own[...] + other[...]
     high = both.astype(jnp.bfloat16)
     low = (both - high.astype(jnp.float32)).astype(jnp.bfloat16)
-    mine = proj + lax.axis_index("tensor") * 2 * half
+    mine = lax.axis_index("tensor") * 2 * half
     left = lax.broadcasted_iota(jnp.int32, (half, LANES), 1) < proj
     for s in range(seqs):
         at = slice(s * length, (s + 1) * length)
         h, l = high[at], low[at]
         grams[s] = lax.dot_general(
-            jnp.concatenate([h, l, h], axis=0),
+            jnp.concatenate([h, l, h], axis=0)[:, :proj],
             jnp.concatenate([h, h, l], axis=0),
             (((0,), (0,)), ((), ())),
             preferred_element_type=jnp.float32,
         )
-    fetch.wait()
     for s in range(seqs):
         even = grams[s, pl.ds(mine, half, stride=2), :]
         odd = grams[s, pl.ds(mine + 1, half, stride=2), :]
-        feature = jnp.where(left, even, pltpu.roll(odd, proj, 1)).astype(out.dtype)
-        group = s // share
-
-        def place(k, s=s, group=group, feature=feature):
-            named = domains[k, s]
-            out[named, group * CAP + rank(domains, s, group * share, named)] = feature
+        feature = jnp.where(left, pltpu.roll(even, proj, 1), odd).astype(out.dtype)
+
+        def place(k, s=s, feature=feature):
+            slot = table[k, s]
+            out[slot // out.shape[1], slot % out.shape[1]] = feature
 
         each(fanout, place)
 
 
-def spread(domains, own, other, share, peers, tensor_count):
-    seqs = domains.shape[1]
+def spread(table, own, other, share, peers, tensor_count):
+    seqs = table.shape[1]
     proj = own.shape[1] // 2
     half = proj * proj // LANES // tensor_count
     return pl.pallas_call(
-        functools.partial(feature_kernel, share),
+        feature_kernel,
         out_shape=jax.ShapeDtypeStruct((peers, seqs // share * CAP, half, LANES), jnp.bfloat16),
-        in_specs=[ANY, VMEM, VMEM],
-        out_specs=VMEM,
-        scratch_shapes=[
-            pltpu.VMEM((seqs, 2 * proj, 2 * proj), jnp.float32),
-            pltpu.SMEM(domains.shape, jnp.int32),
-            pltpu.SemaphoreType.DMA,
-        ],
+        in_specs=[SMEM, VMEM, VMEM],
+        out_specs=VMEM,
+        scratch_shapes=[pltpu.VMEM((seqs, proj, 2 * proj), jnp.float32)],
         compiler_params=room(
             ((4 * own.shape[0], LANES), jnp.float32), ((peers, seqs // share * CAP, half, LANES), jnp.bfloat16)
         ),
         cost_estimate=pl.CostEstimate(flops=50_000_000_000, bytes_accessed=1 << 20, transcendentals=0),
         name="spread",
-    )(domains, *near(own, other))
+    )(table, *near(own, other))
 
 
 def score_kernel(features, own, other, out, rows_v):
@@ -180,54 +172,57 @@
     )(*near(features, own, other))
 
 
-def plan_kernel(share, domains, own, out):
+def plan_kernel(share, domains, own, table):
     del own
-    fanout = domains.shape[0]
-    first = lax.axis_index("tensor") * share
-    column = lax.broadcasted_iota(jnp.int32, (1, out.shape[1]), 1)
-    out[...] = jnp.zeros_like(out)
-    for s in range(share):
-
-        def mark(k, s=s):
-            named = domains[k, first + s]
-            found = jnp.int32(0)
-            for other in range(s):
-                found += sum((domains[j, first + other] == named).astype(jnp.int32) for j in range(fanout))
-            row = 2 * CAP * named + found
-            out[pl.ds(s * fanout + k, 1)] = ((column == row) | (column == row + CAP)).astype(jnp.float32)
-
-        each(fanout, mark)
-
-
-def plan(domains, own, share, count):
-    rows = -(-share * domains.shape[0] // 8) * 8
+    fanout, seqs = domains.shape
+    groups = seqs // share
+    for s in range(seqs):
+
+        def place(k, s=s):
+            named = domains[k, s]
+            group = s // share
+            table[k, s] = (named * groups + group) * CAP + rank(domains, s, group * share, named)
+
+        each(fanout, place)
+
+
+def plan(domains, own, share):
     return pl.pallas_call(
         functools.partial(plan_kernel, share),
-        out_shape=jax.ShapeDtypeStruct((rows, count), jnp.float32),
+        out_shape=pltpu.SMEM(domains.shape, jnp.int32),
         in_specs=[SMEM, ANY],
-        out_specs=VMEM,
-        compiler_params=room(((rows, max(count, LANES)), jnp.float32)),
+        out_specs=SMEM,
+        compiler_params=room(),
         name="plan",
     )(domains, own)
 
 
-def pick_kernel(chosen, scores, out):
+def pick_kernel(table, scores, out):
     share, fanout, _ = out.shape
-    rows = jnp.concatenate([scores[p] for p in range(scores.shape[0])], axis=0)
-    picked = jnp.dot(chosen[...], rows, precision=lax.Precision.HIGHEST, preferred_element_type=jnp.float32)
+    halves = table.shape[1] // share
+    first = lax.axis_index("tensor") * share
     for s in range(share):
-        out[s] = picked[s * fanout : (s + 1) * fanout]
-
-
-def pick(chosen, scores, share, fanout):
+
+        def take(k, s=s):
+            slot = table[k, first + s]
+            at = slot // (halves * CAP) * halves
+            both = scores[at]
+            for half in range(1, halves):
+                both = both + scores[at + half]
+            out[s, pl.ds(k, 1)] = jnp.where(slot % CAP == 0, both[0:1], both[1:2])
+
+        each(fanout, take)
+
+
+def pick(table, scores, share):
     return pl.pallas_call(
         pick_kernel,
-        out_shape=jax.ShapeDtypeStruct((share, fanout, scores.shape[2]), jnp.float32),
-        in_specs=[VMEM, VMEM],
-        out_specs=VMEM,
-        compiler_params=room((scores.shape, jnp.float32), (scores.shape, jnp.float32), (chosen.shape, jnp.float32)),
+        out_shape=jax.ShapeDtypeStruct((share, table.shape[0], scores.shape[2]), jnp.float32),
+        in_specs=[SMEM, VMEM],
+        out_specs=VMEM,
+        compiler_params=room((scores.shape, jnp.float32), ((8 * share, table.shape[0], scores.shape[2]), jnp.float32)),
         name="pick",
-    )(*near(chosen, scores))
+    )(table, *near(scores))
 
 
 def body(activations, out_grads, proj_in, proj_out, queries, domains):
@@ -241,14 +236,14 @@
     )
     domains = domains.T
     other = lax.ppermute(own, "tensor", swap)
-    chosen = plan(domains, own, share, peers * tensor_count * CAP)
-    queries, chosen = lax.optimization_barrier((queries, chosen))
+    table = plan(domains, own, share)
+    queries, table = lax.optimization_barrier((queries, table))
     other_queries = lax.ppermute(queries, "tensor", swap)
-    sent = spread(domains, own, other, share, peers, tensor_count)
+    sent = spread(table, own, other, share, peers, tensor_count)
     came = lax.all_to_all(sent, "dp", split_axis=0, concat_axis=0, tiled=True)
     scores = score(came, queries, other_queries)
     back = lax.all_to_all(scores, ("dp", "tensor"), split_axis=0, concat_axis=0, tiled=True)
-    return pick(chosen, back, share, domains.shape[0])
+    return pick(table, back, share)
 
 
 def solution(mesh):

time: 30 us -> 29.6 us (0.987)
  Pallas kernels: 5.19 us -> 4.77 us
    pallas_call x3, Pallas kernels: 2 us -> 1.57 us  [the longest x1 0.64 us: pick(): pl.pallas_call(pick_kernel, out_shape=jax.ShapeDtypeStruct((share, table....]
  transfers between devices with their start and end apart: 2 -> 2, of which waited for: 1 -> 1; matrix products, arithmetic and copies ran while one was open for 0% -> 0% of each run, Pallas kernels for 4% -> 3%
where the time goes in v6:
time: 29.6 us; the launch traced here: 29.4 us
  blocking collectives  23.6 us (80%)
  Pallas kernels  4.77 us (16%)
  starting transfers between devices  0.64 us (2%)
    all_to_all x1, blocking collectives, body(): came = lax.all_to_all(sent, 'dp', split_axis=0, concat_axis=0, tiled=True)  14.3 us
    all_to_all x1, blocking collectives, body(): lax.all_to_all(scores, ('dp', 'tensor'), split_axis=0, concat_axis=0, til...  9.34 us
    pallas_call x1, Pallas kernels, project(): pl.pallas_call(project_kernel, out_shape=jax.ShapeDtypeStruct((rows, 2 *...  2.52 us
    pallas_call x1, Pallas kernels, score(): pl.pallas_call(score_kernel, out_shape=jax.ShapeDtypeStruct((peers * slot...  0.68 us
    pallas_call x1, Pallas kernels, pick(): pl.pallas_call(pick_kernel, out_shape=jax.ShapeDtypeStruct((share, table....  0.64 us
  transfers between devices with their start and end apart: 2, of which 1 were waited for; matrix products, arithmetic and copies ran while one was open for 0% of the time, Pallas kernels for 3%

profile of v6, /device:TPU:0, one launch (start us, length us, event | category | flops | bytes accessed | tf_op | source)
XLA Modules:
  0.0 29.4 jit_solution(1729601703663547281)
XLA Ops:
  0.0 0.0 copy-start.1
  0.0 0.0 copy-start
  0.0 2.5 %project.1.own = f32[288,128]{1,0:T(8,128)S(1)} custom-call(bf16[288,2048]{1,0:T(8,128)(2,1)} %bitcast.6, bf16[288,2048]{1,0:T(8,128)(2,1)} %bitcast.7, bf16[64,2048]{1,0:T(8,128)(2,1)} %bitcast.8, bf16[64,2048]{1,0:T(8,128)(2,1)} %bitcast.9), custom_call_target="tpu_custom_call" | custom-call | tf_op jit(solution)/shard_map/project/pallas_call | solution.py:59
  2.5 0.5 %collective-permute-start = (f32[288,128]{1,0:T(8,128)S(1)}, f32[288,128]{1,0:T(8,128)S(1)}, u32[]{:S(2)}, u32[]{:S(2)}) collective-permute-start(f32[288,128]{1,0:T(8,128)S(1)} %project.1.own), channel_id=1, source_target_pairs={{0,1},{1,0},{2,3},{3,2},{4,5},{5,4},{6,7},{7,6},{8,9},{9,8},{10,11... | collective-permute-start | bytes 442376 | tf_op jit(solution)/shard_map/ppermute | solution.py:238
  3.0 0.0 copy-done.1
  3.1 0.6 %plan.1.table = s32[2,6]{1,0:T(2,128)S(4)} custom-call(s32[2,6]{1,0:T(2,128)S(1)} %bitcast.5, f32[288,128]{1,0:T(8,128)S(1)} %project.1.own), custom_call_target="tpu_custom_call" | custom-call | tf_op jit(solution)/shard_map/plan/pallas_call | solution.py:190
  3.6 0.0 copy-done
  3.7 0.1 collective-permute-start.1
  3.8 0.3 collective-permute-done.other
  4.1 0.3 %spread.1 = bf16[8,4,16,128]{3,2,1,0:T(8,128)(2,1)S(1)} custom-call(s32[2,6]{1,0:T(2,128)S(4)} %plan.1.table, f32[288,128]{1,0:T(8,128)S(1)} %project.1.own, f32[288,128]{1,0:T(8,128)S(1)} %collective-permute-done.other), custom_call_target="tpu_custom_call" | custom-call | flops 49999998976 | bytes 1048576 | tf_op jit(solution)/shard_map/spread/pallas_call | solution.py:125
  4.4 14.3 %all_to_all.10.features = bf16[8,4,16,128]{3,2,1,0:T(8,128)(2,1)S(1)} all-to-all(bf16[8,4,16,128]{3,2,1,0:T(8,128)(2,1)S(1)} %spread.1), channel_id=1, replica_groups=mesh['groups'=2,'dp'=8,'tensor'=2] {'dp'}, dimensions={0} | all-to-all | bytes 262144 | tf_op jit(solution)/shard_map/all_to_all | solution.py:243
  18.7 0.0 collective-permute-done.1.other
  18.7 0.7 %score.1 = f32[16,2,384]{2,1,0:T(2,128)S(1)} custom-call(bf16[8,4,16,128]{3,2,1,0:T(8,128)(2,1)S(1)} %all_to_all.10.features, bf16[192,4096]{1,0:T(8,128)(2,1)S(1)} %copy-done, bf16[192,4096]{1,0:T(8,128)(2,1)S(1)} %collective-permute-done.1.other), custom_call_target="tpu_custom_call" | custom-call | tf_op jit(solution)/shard_map/score/pallas_call | solution.py:159
  19.4 9.3 %all_to_all.11.scores = f32[16,2,384]{2,1,0:T(2,128)S(1)} all-to-all(f32[16,2,384]{2,1,0:T(2,128)S(1)} %score.1), channel_id=1, replica_groups=mesh['groups'=2,'dp'=8,'tensor'=2] {'dp','tensor'}, dimensions={0} | all-to-all | bytes 98304 | tf_op jit(solution)/shard_map/all_to_all | solution.py:245
  28.7 0.6 %pick.1 = f32[3,2,384]{2,1,0:T(2,128)} custom-call(s32[2,6]{1,0:T(2,128)S(4)} %plan.1.table, f32[16,2,384]{2,1,0:T(2,128)S(1)} %all_to_all.11.scores), custom_call_target="tpu_custom_call" | custom-call | tf_op jit(solution)/shard_map/pick/pallas_call | solution.py:218
Async XLA Ops:
  0.0 3.1 %copy-start.1 = (s32[6,2]{0,1:T(2,128)S(1)}, s32[6,2]{0,1:T(2,128)}, u32[]{:S(2)}) copy-start(s32[6,2]{0,1:T(2,128)} %param.11) | copy-start | bytes 148
  0.0 3.6 %copy-start = (bf16[192,4096]{1,0:T(8,128)(2,1)S(1)}, bf16[192,4096]{1,0:T(8,128)(2,1)}, u32[]{:S(2)}) copy-start(bf16[192,4096]{1,0:T(8,128)(2,1)} %own) | copy-start | bytes 4718596
  2.5 1.5 %collective-permute-start = (f32[288,128]{1,0:T(8,128)S(1)}, f32[288,128]{1,0:T(8,128)S(1)}, u32[]{:S(2)}, u32[]{:S(2)}) collective-permute-start(f32[288,128]{1,0:T(8,128)S(1)} %project.1.own), channel_id=1, source_target_pairs={{0,1},{1,0},{2,3},{3,2},{4,5},{5,4},{6,7},{7,6},{8,9},{9,8},{10,11... | collective-permute-start | bytes 442376 | tf_op jit(solution)/shard_map/ppermute | solution.py:238
  3.7 15.0 %collective-permute-start.1 = (bf16[192,4096]{1,0:T(8,128)(2,1)S(1)}, bf16[192,4096]{1,0:T(8,128)(2,1)S(1)}, u32[]{:S(2)}, u32[]{:S(2)}) collective-permute-start(bf16[192,4096]{1,0:T(8,128)(2,1)S(1)} %copy-done), channel_id=1, source_target_pairs={{0,1},{1,0},{2,3},{3,2},{4,5},{5,4},{6,7},{7,6},{8,9},{9,8},{10,11... | collective-permute-start | bytes 4718600 | tf_op jit(solution)/shard_map/ppermute | solution.py:241

commit v7 on v6

--- a/solution.py
+++ b/solution.py
@@ -15,6 +15,10 @@
 VMEM = pl.BlockSpec(memory_space=pltpu.VMEM)
 SMEM = pl.BlockSpec(memory_space=pltpu.SMEM)
 ANY = pl.BlockSpec(memory_space=pl.ANY)
+
+
+def turned(count, first):
+    return [(first + i) % count for i in range(count)]
 
 
 def each(count, step):
@@ -151,7 +155,7 @@
     )
     scores = jnp.concatenate([jnp.where(me == 0, mine, theirs), jnp.where(me == 0, theirs, mine)], axis=1)
     for p in range(out.shape[0]):
-        out[p] = scores[p * CAP : (p + 1) * CAP]
+        out[(p - 1) % out.shape[0]] = scores[p * CAP : (p + 1) * CAP]
 
 
 def score(features, own, other):
@@ -172,7 +176,7 @@
     )(*near(features, own, other))
 
 
-def plan_kernel(share, domains, own, table):
+def plan_kernel(share, peers, meet, domains, own, table):
     del own
     fanout, seqs = domains.shape
     groups = seqs // share
@@ -181,14 +185,15 @@
         def place(k, s=s):
             named = domains[k, s]
             group = s // share
-            table[k, s] = (named * groups + group) * CAP + rank(domains, s, group * share, named)
+            owner = (named + peers - meet) % peers
+            table[k, s] = (owner * groups + group) * CAP + rank(domains, s, group * share, named)
 
         each(fanout, place)
 
 
-def plan(domains, own, share):
-    return pl.pallas_call(
-        functools.partial(plan_kernel, share),
+def plan(domains, own, share, peers, meet):
+    return pl.pallas_call(
+        functools.partial(plan_kernel, share, peers, meet),
         out_shape=pltpu.SMEM(domains.shape, jnp.int32),
         in_specs=[SMEM, ANY],
         out_specs=SMEM,
@@ -205,10 +210,10 @@
 
         def take(k, s=s):
             slot = table[k, first + s]
-            at = slot // (halves * CAP) * halves
-            both = scores[at]
+            at = slot // (halves * CAP) * halves + scores.shape[0] - 1
+            both = scores[at % scores.shape[0]]
             for half in range(1, halves):
-                both = both + scores[at + half]
+                both = both + scores[(at + half) % scores.shape[0]]
             out[s, pl.ds(k, 1)] = jnp.where(slot % CAP == 0, both[0:1], both[1:2])
 
         each(fanout, take)
@@ -231,18 +236,24 @@
     tensor_count = lax.axis_size("tensor")
     share = seqs // tensor_count
     swap = [(i, i ^ 1) for i in range(tensor_count)]
+    meet = (peers // 2 + 1) % peers
     own = project(
         activations.reshape(seqs * length, width), out_grads.reshape(seqs * length, width), proj_in.T, proj_out.T
     )
     domains = domains.T
     other = lax.ppermute(own, "tensor", swap)
-    table = plan(domains, own, share)
+    table = plan(domains, own, share, peers, meet)
     queries, table = lax.optimization_barrier((queries, table))
     other_queries = lax.ppermute(queries, "tensor", swap)
     sent = spread(table, own, other, share, peers, tensor_count)
-    came = lax.all_to_all(sent, "dp", split_axis=0, concat_axis=0, tiled=True)
+    came = lax.all_to_all(
+        sent, "dp", split_axis=0, concat_axis=0, tiled=True, axis_index_groups=[turned(peers, meet)]
+    )
     scores = score(came, queries, other_queries)
-    back = lax.all_to_all(scores, ("dp", "tensor"), split_axis=0, concat_axis=0, tiled=True)
+    devices = turned(peers * tensor_count, meet * tensor_count + 1)
+    back = lax.all_to_all(
+        scores, ("dp", "tensor"), split_axis=0, concat_axis=0, tiled=True, axis_index_groups=[devices]
+    )
     return pick(table, back, share)
 
 

time: 29.6 us -> 26.1 us (0.88)
  blocking collectives: 23.6 us -> 20.1 us
    all_to_all x1, blocking collectives: 14.3 us -> 11.9 us  [body(): lax.all_to_all(sent, 'dp', split_axis=0, concat_axis=0, tiled=True, axis_...]
    all_to_all x1, blocking collectives: 9.34 us -> 8.22 us  [body(): lax.all_to_all(scores, ('dp', 'tensor'), split_axis=0, concat_axis=0, til...]
  transfers between devices with their start and end apart: 2 -> 2, of which waited for: 1 -> 1; matrix products, arithmetic and copies ran while one was open for 0% -> 0% of each run, Pallas kernels for 3% -> 4%
where the time goes in v7:
time: 26.1 us; the launch traced here: 25.9 us
  blocking collectives  20.1 us (77%)
  Pallas kernels  4.83 us (19%)
  starting transfers between devices  0.64 us (2%)
    all_to_all x1, blocking collectives, body(): lax.all_to_all(sent, 'dp', split_axis=0, concat_axis=0, tiled=True, axis_...  11.9 us
    all_to_all x1, blocking collectives, body(): lax.all_to_all(scores, ('dp', 'tensor'), split_axis=0, concat_axis=0, til...  8.22 us
    pallas_call x1, Pallas kernels, project(): pl.pallas_call(project_kernel, out_shape=jax.ShapeDtypeStruct((rows, 2 *...  2.52 us
    pallas_call x1, Pallas kernels, score(): pl.pallas_call(score_kernel, out_shape=jax.ShapeDtypeStruct((peers * slot...  0.68 us
    pallas_call x1, Pallas kernels, pick(): pl.pallas_call(pick_kernel, out_shape=jax.ShapeDtypeStruct((share, table....  0.67 us
    pallas_call x1, Pallas kernels, plan(): pl.pallas_call(functools.partial(plan_kernel, share, peers, meet), out_sh...  0.62 us
  transfers between devices with their start and end apart: 2, of which 1 were waited for; matrix products, arithmetic and copies ran while one was open for 0% of the time, Pallas kernels for 4%

profile of v7, /device:TPU:0, one launch (start us, length us, event | category | flops | bytes accessed | tf_op | source)
XLA Modules:
  0.0 25.9 jit_solution(2924857454554720389)
XLA Ops:
  0.0 0.0 copy-start.1
  0.0 0.0 copy-start
  0.0 2.5 %project.1.own = f32[288,128]{1,0:T(8,128)S(1)} custom-call(bf16[288,2048]{1,0:T(8,128)(2,1)} %bitcast.6, bf16[288,2048]{1,0:T(8,128)(2,1)} %bitcast.7, bf16[64,2048]{1,0:T(8,128)(2,1)} %bitcast.8, bf16[64,2048]{1,0:T(8,128)(2,1)} %bitcast.9), custom_call_target="tpu_custom_call" | custom-call | tf_op jit(solution)/shard_map/project/pallas_call | solution.py:63
  2.5 0.5 %collective-permute-start = (f32[288,128]{1,0:T(8,128)S(1)}, f32[288,128]{1,0:T(8,128)S(1)}, u32[]{:S(2)}, u32[]{:S(2)}) collective-permute-start(f32[288,128]{1,0:T(8,128)S(1)} %project.1.own), channel_id=1, source_target_pairs={{0,1},{1,0},{2,3},{3,2},{4,5},{5,4},{6,7},{7,6},{8,9},{9,8},{10,11... | collective-permute-start | bytes 442376 | tf_op jit(solution)/shard_map/ppermute | solution.py:244
  3.0 0.0 copy-done.1
  3.1 0.6 %plan.1.table = s32[2,6]{1,0:T(2,128)S(4)} custom-call(s32[2,6]{1,0:T(2,128)S(1)} %bitcast.5, f32[288,128]{1,0:T(8,128)S(1)} %project.1.own), custom_call_target="tpu_custom_call" | custom-call | tf_op jit(solution)/shard_map/plan/pallas_call | solution.py:195
  3.7 0.0 copy-done
  3.7 0.1 collective-permute-start.1
  3.8 0.2 collective-permute-done.other
  4.1 0.3 %spread.1 = bf16[8,4,16,128]{3,2,1,0:T(8,128)(2,1)S(1)} custom-call(s32[2,6]{1,0:T(2,128)S(4)} %plan.1.table, f32[288,128]{1,0:T(8,128)S(1)} %project.1.own, f32[288,128]{1,0:T(8,128)S(1)} %collective-permute-done.other), custom_call_target="tpu_custom_call" | custom-call | flops 49999998976 | bytes 1048576 | tf_op jit(solution)/shard_map/spread/pallas_call | solution.py:129
  4.4 11.9 %all_to_all.10.features = bf16[8,4,16,128]{3,2,1,0:T(8,128)(2,1)S(1)} all-to-all(bf16[8,4,16,128]{3,2,1,0:T(8,128)(2,1)S(1)} %spread.1), channel_id=1, replica_groups={{10,12,14,0,2,4,6,8},{11,13,15,1,3,5,7,9},{26,28,30,16,18,20,22,24},{27..., dimensions={0} | all-to-all | bytes 262144 | tf_op jit(solution)/shard_map/all_to_all | solution.py:249
  16.3 0.0 collective-permute-done.1.other
  16.3 0.7 %score.1 = f32[16,2,384]{2,1,0:T(2,128)S(1)} custom-call(bf16[8,4,16,128]{3,2,1,0:T(8,128)(2,1)S(1)} %all_to_all.10.features, bf16[192,4096]{1,0:T(8,128)(2,1)S(1)} %copy-done, bf16[192,4096]{1,0:T(8,128)(2,1)S(1)} %collective-permute-done.1.other), custom_call_target="tpu_custom_call" | custom-call | tf_op jit(solution)/shard_map/score/pallas_call | solution.py:163
  17.0 8.2 %all_to_all.11.scores = f32[16,2,384]{2,1,0:T(2,128)S(1)} all-to-all(f32[16,2,384]{2,1,0:T(2,128)S(1)} %score.1), channel_id=1, replica_groups={{11,12,13,14,15,0,1,2,3,4,5,6,7,8,9,10},{27,28,29,30,31,16,17,18,19,20,..., dimensions={0} | all-to-all | bytes 98304 | tf_op jit(solution)/shard_map/all_to_all | solution.py:254
  25.2 0.7 %pick.1 = f32[3,2,384]{2,1,0:T(2,128)} custom-call(s32[2,6]{1,0:T(2,128)S(4)} %plan.1.table, f32[16,2,384]{2,1,0:T(2,128)S(1)} %all_to_all.11.scores), custom_call_target="tpu_custom_call" | custom-call | tf_op jit(solution)/shard_map/pick/pallas_call | solution.py:223
Async XLA Ops:
  0.0 3.1 %copy-start.1 = (s32[6,2]{0,1:T(2,128)S(1)}, s32[6,2]{0,1:T(2,128)}, u32[]{:S(2)}) copy-start(s32[6,2]{0,1:T(2,128)} %param.11) | copy-start | bytes 148
  0.0 3.7 %copy-start = (bf16[192,4096]{1,0:T(8,128)(2,1)S(1)}, bf16[192,4096]{1,0:T(8,128)(2,1)}, u32[]{:S(2)}) copy-start(bf16[192,4096]{1,0:T(8,128)(2,1)} %own) | copy-start | bytes 4718596
  2.5 1.5 %collective-permute-start = (f32[288,128]{1,0:T(8,128)S(1)}, f32[288,128]{1,0:T(8,128)S(1)}, u32[]{:S(2)}, u32[]{:S(2)}) collective-permute-start(f32[288,128]{1,0:T(8,128)S(1)} %project.1.own), channel_id=1, source_target_pairs={{0,1},{1,0},{2,3},{3,2},{4,5},{5,4},{6,7},{7,6},{8,9},{9,8},{10,11... | collective-permute-start | bytes 442376 | tf_op jit(solution)/shard_map/ppermute | solution.py:244
  3.7 12.6 %collective-permute-start.1 = (bf16[192,4096]{1,0:T(8,128)(2,1)S(1)}, bf16[192,4096]{1,0:T(8,128)(2,1)S(1)}, u32[]{:S(2)}, u32[]{:S(2)}) collective-permute-start(bf16[192,4096]{1,0:T(8,128)(2,1)S(1)} %copy-done), channel_id=1, source_target_pairs={{0,1},{1,0},{2,3},{3,2},{4,5},{5,4},{6,7},{7,6},{8,9},{9,8},{10,11... | collective-permute-start | bytes 4718600 | tf_op jit(solution)/shard_map/ppermute | solution.py:247

commit v8 on v7

--- a/solution.py
+++ b/solution.py
@@ -15,6 +15,15 @@
 VMEM = pl.BlockSpec(memory_space=pltpu.VMEM)
 SMEM = pl.BlockSpec(memory_space=pltpu.SMEM)
 ANY = pl.BlockSpec(memory_space=pl.ANY)
+
+
+def half_of(index, core, peers):
+    return core ^ (index >= peers // 2)
+
+
+def my_half(peers):
+    past = (lax.axis_index("dp") >= peers // 2).astype(jnp.int32)
+    return lax.axis_index("tensor") ^ past
 
 
 def turned(count, first):
@@ -99,7 +108,7 @@
     both = own[...] + other[...]
     high = both.astype(jnp.bfloat16)
     low = (both - high.astype(jnp.float32)).astype(jnp.bfloat16)
-    mine = lax.axis_index("tensor") * 2 * half
+    mine = my_half(out.shape[0]) * 2 * half
     left = lax.broadcasted_iota(jnp.int32, (half, LANES), 1) < proj
     for s in range(seqs):
         at = slice(s * length, (s + 1) * length)
@@ -140,7 +149,7 @@
     )(table, *near(own, other))
 
 
-def score_kernel(features, own, other, out, rows_v):
+def score_kernel(meet, features, own, other, out, rows_v):
     peers, slots, half, _ = features.shape
     count = peers * slots
     rows_v[...] = features[...].reshape(count * half, LANES).astype(jnp.float32)
@@ -148,20 +157,21 @@
         [rows_v[pl.ds(c, count, stride=half), :].astype(jnp.bfloat16) for c in range(half)], axis=1
     )
     me = lax.axis_index("tensor")
-    part = pl.ds(pl.multiple_of(me * half * LANES, LANES), half * LANES)
+    part = pl.ds(pl.multiple_of(my_half(peers) * half * LANES, LANES), half * LANES)
     mine, theirs = (
         lax.dot_general(rows, q[:, part], LAST, preferred_element_type=jnp.float32)
         for q in (own, other)
     )
     scores = jnp.concatenate([jnp.where(me == 0, mine, theirs), jnp.where(me == 0, theirs, mine)], axis=1)
-    for p in range(out.shape[0]):
-        out[(p - 1) % out.shape[0]] = scores[p * CAP : (p + 1) * CAP]
-
-
-def score(features, own, other):
+    devices = out.shape[0]
+    for p in range(devices):
+        out[(p + devices // peers * meet + 1) % devices] = scores[p * CAP : (p + 1) * CAP]
+
+
+def score(features, own, other, meet):
     peers, slots, half, _ = features.shape
     return pl.pallas_call(
-        score_kernel,
+        functools.partial(score_kernel, meet),
         out_shape=jax.ShapeDtypeStruct((peers * slots // CAP, CAP, 2 * own.shape[0]), jnp.float32),
         in_specs=[VMEM] * 3,
         out_specs=VMEM,
@@ -202,7 +212,7 @@
     )(domains, own)
 
 
-def pick_kernel(table, scores, out):
+def pick_kernel(meet, table, scores, out):
     share, fanout, _ = out.shape
     halves = table.shape[1] // share
     first = lax.axis_index("tensor") * share
@@ -210,7 +220,7 @@
 
         def take(k, s=s):
             slot = table[k, first + s]
-            at = slot // (halves * CAP) * halves + scores.shape[0] - 1
+            at = (slot // (halves * CAP) + meet) * halves + 1
             both = scores[at % scores.shape[0]]
             for half in range(1, halves):
                 both = both + scores[(at + half) % scores.shape[0]]
@@ -219,9 +229,9 @@
         each(fanout, take)
 
 
-def pick(table, scores, share):
-    return pl.pallas_call(
-        pick_kernel,
+def pick(table, scores, share, meet):
+    return pl.pallas_call(
+        functools.partial(pick_kernel, meet),
         out_shape=jax.ShapeDtypeStruct((share, table.shape[0], scores.shape[2]), jnp.float32),
         in_specs=[SMEM, VMEM],
         out_specs=VMEM,
@@ -246,15 +256,24 @@
     queries, table = lax.optimization_barrier((queries, table))
     other_queries = lax.ppermute(queries, "tensor", swap)
     sent = spread(table, own, other, share, peers, tensor_count)
+    groups = [
+        [index * tensor_count + half_of(index, half, peers) for index in turned(peers, meet)]
+        for half in range(tensor_count)
+    ]
     came = lax.all_to_all(
-        sent, "dp", split_axis=0, concat_axis=0, tiled=True, axis_index_groups=[turned(peers, meet)]
-    )
-    scores = score(came, queries, other_queries)
-    devices = turned(peers * tensor_count, meet * tensor_count + 1)
+        sent, ("dp", "tensor"), split_axis=0, concat_axis=0, tiled=True, axis_index_groups=groups
+    )
+    scores = score(came, queries, other_queries, meet)
+    devices = peers * tensor_count
     back = lax.all_to_all(
-        scores, ("dp", "tensor"), split_axis=0, concat_axis=0, tiled=True, axis_index_groups=[devices]
-    )
-    return pick(table, back, share)
+        scores,
+        ("dp", "tensor"),
+        split_axis=0,
+        concat_axis=0,
+        tiled=True,
+        axis_index_groups=[turned(devices, devices - 1)],
+    )
+    return pick(table, back, share, meet)
 
 
 def solution(mesh):

time: 26.1 us -> 25.4 us (0.973)
  blocking collectives: 20.1 us -> 19.4 us
    all_to_all x1, blocking collectives: 11.9 us -> 10.7 us  [body(): lax.all_to_all(sent, ('dp', 'tensor'), split_axis=0, concat_axis=0, tiled...]
    all_to_all x1, blocking collectives: 8.22 us -> 8.73 us  [body(): lax.all_to_all(scores, ('dp', 'tensor'), split_axis=0, concat_axis=0, til...]
where the time goes in v8:
time: 25.4 us; the launch traced here: 25.2 us
  blocking collectives  19.4 us (76%)
  Pallas kernels  4.83 us (19%)
  starting transfers between devices  0.64 us (3%)
    all_to_all x1, blocking collectives, body(): lax.all_to_all(sent, ('dp', 'tensor'), split_axis=0, concat_axis=0, tiled...  10.7 us
    all_to_all x1, blocking collectives, body(): lax.all_to_all(scores, ('dp', 'tensor'), split_axis=0, concat_axis=0, til...  8.73 us
    pallas_call x1, Pallas kernels, project(): pl.pallas_call(project_kernel, out_shape=jax.ShapeDtypeStruct((rows, 2 *...  2.52 us
    pallas_call x1, Pallas kernels, score(): pl.pallas_call(functools.partial(score_kernel, meet), out_shape=jax.Shape...  0.68 us
    pallas_call x1, Pallas kernels, pick(): pl.pallas_call(functools.partial(pick_kernel, meet), out_shape=jax.ShapeD...  0.67 us
    pallas_call x1, Pallas kernels, plan(): pl.pallas_call(functools.partial(plan_kernel, share, peers, meet), out_sh...  0.62 us
    ppermute x1, starting transfers between devices, body(): other = lax.ppermute(own, 'tensor', swap)  0.52 us
  transfers between devices with their start and end apart: 2, of which 1 were waited for; matrix products, arithmetic and copies ran while one was open for 0% of the time, Pallas kernels for 4%

profile of v8, /device:TPU:0, one launch (start us, length us, event | category | flops | bytes accessed | tf_op | source)
XLA Modules:
  0.0 25.2 jit_solution(5821587738293912728)
XLA Ops:
  0.0 0.0 copy-start.1
  0.0 0.0 copy-start
  0.0 2.5 %project.1.own = f32[288,128]{1,0:T(8,128)S(1)} custom-call(bf16[288,2048]{1,0:T(8,128)(2,1)} %bitcast.6, bf16[288,2048]{1,0:T(8,128)(2,1)} %bitcast.7, bf16[64,2048]{1,0:T(8,128)(2,1)} %bitcast.8, bf16[64,2048]{1,0:T(8,128)(2,1)} %bitcast.9), custom_call_target="tpu_custom_call" | custom-call | tf_op jit(solution)/shard_map/project/pallas_call | solution.py:72
  2.5 0.5 %collective-permute-start = (f32[288,128]{1,0:T(8,128)S(1)}, f32[288,128]{1,0:T(8,128)S(1)}, u32[]{:S(2)}, u32[]{:S(2)}) collective-permute-start(f32[288,128]{1,0:T(8,128)S(1)} %project.1.own), channel_id=1, source_target_pairs={{0,1},{1,0},{2,3},{3,2},{4,5},{5,4},{6,7},{7,6},{8,9},{9,8},{10,11... | collective-permute-start | bytes 442376 | tf_op jit(solution)/shard_map/ppermute | solution.py:254
  3.0 0.0 copy-done.1
  3.1 0.6 %plan.1.table = s32[2,6]{1,0:T(2,128)S(4)} custom-call(s32[2,6]{1,0:T(2,128)S(1)} %bitcast.5, f32[288,128]{1,0:T(8,128)S(1)} %project.1.own), custom_call_target="tpu_custom_call" | custom-call | tf_op jit(solution)/shard_map/plan/pallas_call | solution.py:205
  3.7 0.0 copy-done
  3.7 0.1 collective-permute-start.1
  3.8 0.2 collective-permute-done.other
  4.1 0.3 %spread.1 = bf16[8,4,16,128]{3,2,1,0:T(8,128)(2,1)S(1)} custom-call(s32[2,6]{1,0:T(2,128)S(4)} %plan.1.table, f32[288,128]{1,0:T(8,128)S(1)} %project.1.own, f32[288,128]{1,0:T(8,128)S(1)} %collective-permute-done.other), custom_call_target="tpu_custom_call" | custom-call | flops 49999998976 | bytes 1048576 | tf_op jit(solution)/shard_map/spread/pallas_call | solution.py:138
  4.4 10.7 %all_to_all.10.features = bf16[8,4,16,128]{3,2,1,0:T(8,128)(2,1)S(1)} all-to-all(bf16[8,4,16,128]{3,2,1,0:T(8,128)(2,1)S(1)} %spread.1), channel_id=1, replica_groups={{11,13,15,0,2,4,6,9},{10,12,14,1,3,5,7,8},{27,29,31,16,18,20,22,25},{26..., dimensions={0} | all-to-all | bytes 262144 | tf_op jit(solution)/shard_map/all_to_all | solution.py:263
  15.1 0.0 collective-permute-done.1.other
  15.1 0.7 %score.1 = f32[16,2,384]{2,1,0:T(2,128)S(1)} custom-call(bf16[8,4,16,128]{3,2,1,0:T(8,128)(2,1)S(1)} %all_to_all.10.features, bf16[192,4096]{1,0:T(8,128)(2,1)S(1)} %copy-done, bf16[192,4096]{1,0:T(8,128)(2,1)S(1)} %collective-permute-done.1.other), custom_call_target="tpu_custom_call" | custom-call | tf_op jit(solution)/shard_map/score/pallas_call | solution.py:173
  15.8 8.7 %all_to_all.11.scores = f32[16,2,384]{2,1,0:T(2,128)S(1)} all-to-all(f32[16,2,384]{2,1,0:T(2,128)S(1)} %score.1), channel_id=1, replica_groups={{15,0,1,2,3,4,5,6,7,8,9,10,11,12,13,14},{31,16,17,18,19,20,21,22,23,24,..., dimensions={0} | all-to-all | bytes 98304 | tf_op jit(solution)/shard_map/all_to_all | solution.py:268
  24.5 0.7 %pick.1 = f32[3,2,384]{2,1,0:T(2,128)} custom-call(s32[2,6]{1,0:T(2,128)S(4)} %plan.1.table, f32[16,2,384]{2,1,0:T(2,128)S(1)} %all_to_all.11.scores), custom_call_target="tpu_custom_call" | custom-call | tf_op jit(solution)/shard_map/pick/pallas_call | solution.py:233
Async XLA Ops:
  0.0 3.1 %copy-start.1 = (s32[6,2]{0,1:T(2,128)S(1)}, s32[6,2]{0,1:T(2,128)}, u32[]{:S(2)}) copy-start(s32[6,2]{0,1:T(2,128)} %param.11) | copy-start | bytes 148
  0.0 3.7 %copy-start = (bf16[192,4096]{1,0:T(8,128)(2,1)S(1)}, bf16[192,4096]{1,0:T(8,128)(2,1)}, u32[]{:S(2)}) copy-start(bf16[192,4096]{1,0:T(8,128)(2,1)} %own) | copy-start | bytes 4718596
  2.5 1.5 %collective-permute-start = (f32[288,128]{1,0:T(8,128)S(1)}, f32[288,128]{1,0:T(8,128)S(1)}, u32[]{:S(2)}, u32[]{:S(2)}) collective-permute-start(f32[288,128]{1,0:T(8,128)S(1)} %project.1.own), channel_id=1, source_target_pairs={{0,1},{1,0},{2,3},{3,2},{4,5},{5,4},{6,7},{7,6},{8,9},{9,8},{10,11... | collective-permute-start | bytes 442376 | tf_op jit(solution)/shard_map/ppermute | solution.py:254
  3.7 11.4 %collective-permute-start.1 = (bf16[192,4096]{1,0:T(8,128)(2,1)S(1)}, bf16[192,4096]{1,0:T(8,128)(2,1)S(1)}, u32[]{:S(2)}, u32[]{:S(2)}) collective-permute-start(bf16[192,4096]{1,0:T(8,128)(2,1)S(1)} %copy-done), channel_id=1, source_target_pairs={{0,1},{1,0},{2,3},{3,2},{4,5},{5,4},{6,7},{7,6},{8,9},{9,8},{10,11... | collective-permute-start | bytes 4718600 | tf_op jit(solution)/shard_map/ppermute | solution.py:257

commit v9 on v8

--- a/solution.py
+++ b/solution.py
@@ -114,8 +114,8 @@
         at = slice(s * length, (s + 1) * length)
         h, l = high[at], low[at]
         grams[s] = lax.dot_general(
-            jnp.concatenate([h, l, h], axis=0)[:, :proj],
-            jnp.concatenate([h, h, l], axis=0),
+            jnp.concatenate([h, l, h, l], axis=0)[:, :proj],
+            jnp.concatenate([h, h, l, l], axis=0),
             (((0,), (0,)), ((), ())),
             preferred_element_type=jnp.float32,
         )
@@ -159,10 +159,10 @@
     me = lax.axis_index("tensor")
     part = pl.ds(pl.multiple_of(my_half(peers) * half * LANES, LANES), half * LANES)
     mine, theirs = (
-        lax.dot_general(rows, q[:, part], LAST, preferred_element_type=jnp.float32)
+        lax.dot_general(q[:, part], rows, LAST, preferred_element_type=jnp.float32)
         for q in (own, other)
     )
-    scores = jnp.concatenate([jnp.where(me == 0, mine, theirs), jnp.where(me == 0, theirs, mine)], axis=1)
+    scores = jnp.concatenate([jnp.where(me == 0, mine, theirs), jnp.where(me == 0, theirs, mine)], axis=0).T
     devices = out.shape[0]
     for p in range(devices):
         out[(p + devices // peers * meet + 1) % devices] = scores[p * CAP : (p + 1) * CAP]
@@ -253,8 +253,10 @@
     domains = domains.T
     other = lax.ppermute(own, "tensor", swap)
     table = plan(domains, own, share, peers, meet)
-    queries, table = lax.optimization_barrier((queries, table))
+    kept, table = lax.optimization_barrier((queries, table))
+    queries, own = lax.optimization_barrier((queries, own))
     other_queries = lax.ppermute(queries, "tensor", swap)
+    queries = kept
     sent = spread(table, own, other, share, peers, tensor_count)
     groups = [
         [index * tensor_count + half_of(index, half, peers) for index in turned(peers, meet)]

time: 25.4 us -> 25.4 us (level)
  no operation moved by 1% of the time
where the time goes in v9:
time: 25.4 us; the launch traced here: 25.1 us
  blocking collectives  19.4 us (76%)
  Pallas kernels  4.81 us (19%)
  starting transfers between devices  0.6 us (2%)
  waiting for transfers between devices  0.29 us (1%)
    all_to_all x1, blocking collectives, body(): lax.all_to_all(sent, ('dp', 'tensor'), split_axis=0, concat_axis=0, tiled...  10.7 us
    all_to_all x1, blocking collectives, body(): lax.all_to_all(scores, ('dp', 'tensor'), split_axis=0, concat_axis=0, til...  8.73 us
    pallas_call x1, Pallas kernels, project(): pl.pallas_call(project_kernel, out_shape=jax.ShapeDtypeStruct((rows, 2 *...  2.52 us
    pallas_call x1, Pallas kernels, pick(): pl.pallas_call(functools.partial(pick_kernel, meet), out_shape=jax.ShapeD...  0.67 us
    pallas_call x1, Pallas kernels, score(): pl.pallas_call(functools.partial(score_kernel, meet), out_shape=jax.Shape...  0.64 us
    pallas_call x1, Pallas kernels, plan(): pl.pallas_call(functools.partial(plan_kernel, share, peers, meet), out_sh...  0.62 us
    ppermute x1, starting transfers between devices, body(): other = lax.ppermute(own, 'tensor', swap)  0.52 us
  transfers between devices with their start and end apart: 2, of which 1 were waited for; matrix products, arithmetic and copies ran while one was open for 0% of the time, Pallas kernels for 4%

profile of v9, /device:TPU:0, one launch (start us, length us, event | category | flops | bytes accessed | tf_op | source)
XLA Modules:
  0.0 25.1 jit_solution(5910094578062456919)
XLA Ops:
  0.0 0.0 copy-start
  0.0 0.0 copy-start.1
  0.0 2.5 %project.1.own = f32[288,128]{1,0:T(8,128)S(1)} custom-call(bf16[288,2048]{1,0:T(8,128)(2,1)} %bitcast.6, bf16[288,2048]{1,0:T(8,128)(2,1)} %bitcast.7, bf16[64,2048]{1,0:T(8,128)(2,1)} %bitcast.8, bf16[64,2048]{1,0:T(8,128)(2,1)} %bitcast.9), custom_call_target="tpu_custom_call" | custom-call | tf_op jit(solution)/shard_map/project/pallas_call | solution.py:72
  2.5 0.5 %collective-permute-start = (f32[288,128]{1,0:T(8,128)S(1)}, f32[288,128]{1,0:T(8,128)S(1)}, u32[]{:S(2)}, u32[]{:S(2)}) collective-permute-start(f32[288,128]{1,0:T(8,128)S(1)} %project.1.own), channel_id=1, source_target_pairs={{0,1},{1,0},{2,3},{3,2},{4,5},{5,4},{6,7},{7,6},{8,9},{9,8},{10,11... | collective-permute-start | bytes 442376 | tf_op jit(solution)/shard_map/ppermute | solution.py:254
  3.0 0.0 copy-done
  3.1 0.1 collective-permute-start.1
  3.1 0.0 copy-done.1
  3.1 0.6 %plan.1.table = s32[2,6]{1,0:T(2,128)S(4)} custom-call(s32[2,6]{1,0:T(2,128)S(1)} %bitcast.5, f32[288,128]{1,0:T(8,128)S(1)} %project.1.own), custom_call_target="tpu_custom_call" | custom-call | tf_op jit(solution)/shard_map/plan/pallas_call | solution.py:205
  3.8 0.3 %collective-permute-done.other = f32[288,128]{1,0:T(8,128)S(1)} collective-permute-done((f32[288,128]{1,0:T(8,128)S(1)}, f32[288,128]{1,0:T(8,128)S(1)}, u32[]{:S(2)}, u32[]{:S(2)}) %collective-permute-start) | collective-permute-done | bytes 147488 | tf_op jit(solution)/shard_map/ppermute | solution.py:254
  4.1 0.4 %spread.1 = bf16[8,4,16,128]{3,2,1,0:T(8,128)(2,1)S(1)} custom-call(s32[2,6]{1,0:T(2,128)S(4)} %plan.1.table, f32[288,128]{1,0:T(8,128)S(1)} %project.1.own, f32[288,128]{1,0:T(8,128)S(1)} %collective-permute-done.other), custom_call_target="tpu_custom_call" | custom-call | flops 49999998976 | bytes 1048576 | tf_op jit(solution)/shard_map/spread/pallas_call | solution.py:138
  4.4 10.7 %all_to_all.10.features = bf16[8,4,16,128]{3,2,1,0:T(8,128)(2,1)S(1)} all-to-all(bf16[8,4,16,128]{3,2,1,0:T(8,128)(2,1)S(1)} %spread.1), channel_id=1, replica_groups={{11,13,15,0,2,4,6,9},{10,12,14,1,3,5,7,8},{27,29,31,16,18,20,22,25},{26..., dimensions={0} | all-to-all | bytes 262144 | tf_op jit(solution)/shard_map/all_to_all | solution.py:265
  15.1 0.0 collective-permute-done.1.other
  15.1 0.6 %score.1 = f32[16,2,384]{2,1,0:T(2,128)S(1)} custom-call(bf16[8,4,16,128]{3,2,1,0:T(8,128)(2,1)S(1)} %all_to_all.10.features, bf16[192,4096]{1,0:T(8,128)(2,1)S(1)} %copy-done, bf16[192,4096]{1,0:T(8,128)(2,1)S(1)} %collective-permute-done.1.other), custom_call_target="tpu_custom_call" | custom-call | tf_op jit(solution)/shard_map/score/pallas_call | solution.py:173
  15.7 8.7 %all_to_all.11.scores = f32[16,2,384]{2,1,0:T(2,128)S(1)} all-to-all(f32[16,2,384]{2,1,0:T(2,128)S(1)} %score.1), channel_id=1, replica_groups={{15,0,1,2,3,4,5,6,7,8,9,10,11,12,13,14},{31,16,17,18,19,20,21,22,23,24,..., dimensions={0} | all-to-all | bytes 98304 | tf_op jit(solution)/shard_map/all_to_all | solution.py:270
  24.5 0.7 %pick.1 = f32[3,2,384]{2,1,0:T(2,128)} custom-call(s32[2,6]{1,0:T(2,128)S(4)} %plan.1.table, f32[16,2,384]{2,1,0:T(2,128)S(1)} %all_to_all.11.scores), custom_call_target="tpu_custom_call" | custom-call | tf_op jit(solution)/shard_map/pick/pallas_call | solution.py:233
Async XLA Ops:
  0.0 3.0 %copy-start = (bf16[192,4096]{1,0:T(8,128)(2,1)S(1)}, bf16[192,4096]{1,0:T(8,128)(2,1)}, u32[]{:S(2)}) copy-start(bf16[192,4096]{1,0:T(8,128)(2,1)} %own) | copy-start | bytes 4718596
  0.0 3.1 %copy-start.1 = (s32[6,2]{0,1:T(2,128)S(1)}, s32[6,2]{0,1:T(2,128)}, u32[]{:S(2)}) copy-start(s32[6,2]{0,1:T(2,128)} %param.11) | copy-start | bytes 148
  2.5 1.5 %collective-permute-start = (f32[288,128]{1,0:T(8,128)S(1)}, f32[288,128]{1,0:T(8,128)S(1)}, u32[]{:S(2)}, u32[]{:S(2)}) collective-permute-start(f32[288,128]{1,0:T(8,128)S(1)} %project.1.own), channel_id=1, source_target_pairs={{0,1},{1,0},{2,3},{3,2},{4,5},{5,4},{6,7},{7,6},{8,9},{9,8},{10,11... | collective-permute-start | bytes 442376 | tf_op jit(solution)/shard_map/ppermute | solution.py:254
  3.1 12.0 %collective-permute-start.1 = (bf16[192,4096]{1,0:T(8,128)(2,1)S(1)}, bf16[192,4096]{1,0:T(8,128)(2,1)S(1)}, u32[]{:S(2)}, u32[]{:S(2)}) collective-permute-start(bf16[192,4096]{1,0:T(8,128)(2,1)S(1)} %copy-done), channel_id=1, source_target_pairs={{0,1},{1,0},{2,3},{3,2},{4,5},{5,4},{6,7},{7,6},{8,9},{9,8},{10,11... | collective-permute-start | bytes 4718600 | tf_op jit(solution)/shard_map/ppermute | solution.py:258

commit v10 on v9

--- a/solution.py
+++ b/solution.py
@@ -51,18 +51,20 @@
     return pltpu.CompilerParams(vmem_limit_bytes=2 * held + (1 << 20))
 
 
-def project_kernel(acts, grads, p_in, p_out, out, x_v, w_v, sums, sems):
+def project_kernel(acts, grads, p_in, p_out, out, x_v, w_v, sems):
+    proj = p_in.shape[0]
     for side, (x, w) in enumerate(((grads, p_out), (acts, p_in))):
-        pltpu.make_async_copy(w, w_v.at[side], sems.at[side, 0]).start()
+        pltpu.make_async_copy(w, w_v.at[side, pl.ds(side * proj, proj)], sems.at[side, 0]).start()
         pltpu.make_async_copy(x, x_v.at[side], sems.at[side, 1]).start()
+    for side in range(2):
+        w_v[side, pl.ds((1 - side) * proj, proj)] = jnp.zeros(p_in.shape, w_v.dtype)
+    out[...] = jnp.zeros_like(out)
 
     @pl.loop(0, 2)
     def _(side):
-        pltpu.make_async_copy(p_in, w_v.at[side], sems.at[side, 0]).wait()
+        pltpu.make_async_copy(p_in, w_v.at[side, pl.ds(pl.multiple_of(side * proj, proj), proj)], sems.at[side, 0]).wait()
         pltpu.make_async_copy(acts, x_v.at[side], sems.at[side, 1]).wait()
-        sums[side] = lax.dot_general(x_v[side], w_v[side], LAST, preferred_element_type=jnp.float32)
-
-    out[...] = jnp.concatenate([sums[0], sums[1]], axis=1)
+        out[...] += lax.dot_general(x_v[side], w_v[side], LAST, preferred_element_type=jnp.float32)
 
 
 def project(acts, grads, p_in, p_out):
@@ -76,11 +78,10 @@
         out_specs=VMEM,
         scratch_shapes=[
             pltpu.VMEM((2, rows, width), bf16),
-            pltpu.VMEM((2, proj, width), bf16),
-            pltpu.VMEM((2, rows, proj), jnp.float32),
+            pltpu.VMEM((2, 2 * proj, width), bf16),
             pltpu.SemaphoreType.DMA((2, 2)),
         ],
-        compiler_params=room((acts.shape, bf16), (p_in.shape, bf16), ((rows, 4 * LANES), jnp.float32)),
+        compiler_params=room((acts.shape, bf16), ((4 * proj, width), bf16), ((rows, 2 * LANES), jnp.float32)),
         name="project",
     )(*far(acts, grads, p_in, p_out))
 

time: 25.4 us -> 25.3 us (level)
  no operation moved by 1% of the time
where the time goes in v10:
time: 25.3 us; the launch traced here: 25.1 us
  blocking collectives  19.4 us (77%)
  Pallas kernels  4.74 us (19%)
  starting transfers between devices  0.6 us (2%)
  waiting for transfers between devices  0.29 us (1%)
    all_to_all x1, blocking collectives, body(): lax.all_to_all(sent, ('dp', 'tensor'), split_axis=0, concat_axis=0, tiled...  10.7 us
    all_to_all x1, blocking collectives, body(): lax.all_to_all(scores, ('dp', 'tensor'), split_axis=0, concat_axis=0, til...  8.75 us
    pallas_call x1, Pallas kernels, project(): pl.pallas_call(project_kernel, out_shape=jax.ShapeDtypeStruct((rows, 2 *...  2.45 us
    pallas_call x1, Pallas kernels, pick(): pl.pallas_call(functools.partial(pick_kernel, meet), out_shape=jax.ShapeD...  0.67 us
    pallas_call x1, Pallas kernels, score(): pl.pallas_call(functools.partial(score_kernel, meet), out_shape=jax.Shape...  0.64 us
    pallas_call x1, Pallas kernels, plan(): pl.pallas_call(functools.partial(plan_kernel, share, peers, meet), out_sh...  0.62 us
    ppermute x1, starting transfers between devices, body(): other = lax.ppermute(own, 'tensor', swap)  0.52 us
  transfers between devices with their start and end apart: 2, of which 1 were waited for; matrix products, arithmetic and copies ran while one was open for 0% of the time, Pallas kernels for 4%

profile of v10, /device:TPU:0, one launch (start us, length us, event | category | flops | bytes accessed | tf_op | source)
XLA Modules:
  0.0 25.1 jit_solution(13412562502057606405)
XLA Ops:
  0.0 0.0 copy-start
  0.0 0.0 copy-start.1
  0.0 2.5 %project.1.own = f32[288,128]{1,0:T(8,128)S(1)} custom-call(bf16[288,2048]{1,0:T(8,128)(2,1)} %bitcast.6, bf16[288,2048]{1,0:T(8,128)(2,1)} %bitcast.7, bf16[64,2048]{1,0:T(8,128)(2,1)} %bitcast.8, bf16[64,2048]{1,0:T(8,128)(2,1)} %bitcast.9), custom_call_target="tpu_custom_call" | custom-call | tf_op jit(solution)/shard_map/project/pallas_call | solution.py:74
  2.5 0.5 %collective-permute-start = (f32[288,128]{1,0:T(8,128)S(1)}, f32[288,128]{1,0:T(8,128)S(1)}, u32[]{:S(2)}, u32[]{:S(2)}) collective-permute-start(f32[288,128]{1,0:T(8,128)S(1)} %project.1.own), channel_id=1, source_target_pairs={{0,1},{1,0},{2,3},{3,2},{4,5},{5,4},{6,7},{7,6},{8,9},{9,8},{10,11... | collective-permute-start | bytes 442376 | tf_op jit(solution)/shard_map/ppermute | solution.py:255
  3.0 0.0 copy-done
  3.0 0.1 collective-permute-start.1
  3.1 0.0 copy-done.1
  3.1 0.6 %plan.1.table = s32[2,6]{1,0:T(2,128)S(4)} custom-call(s32[2,6]{1,0:T(2,128)S(1)} %bitcast.5, f32[288,128]{1,0:T(8,128)S(1)} %project.1.own), custom_call_target="tpu_custom_call" | custom-call | tf_op jit(solution)/shard_map/plan/pallas_call | solution.py:206
  3.7 0.3 %collective-permute-done.other = f32[288,128]{1,0:T(8,128)S(1)} collective-permute-done((f32[288,128]{1,0:T(8,128)S(1)}, f32[288,128]{1,0:T(8,128)S(1)}, u32[]{:S(2)}, u32[]{:S(2)}) %collective-permute-start) | collective-permute-done | bytes 147488 | tf_op jit(solution)/shard_map/ppermute | solution.py:255
  4.0 0.4 %spread.1 = bf16[8,4,16,128]{3,2,1,0:T(8,128)(2,1)S(1)} custom-call(s32[2,6]{1,0:T(2,128)S(4)} %plan.1.table, f32[288,128]{1,0:T(8,128)S(1)} %project.1.own, f32[288,128]{1,0:T(8,128)S(1)} %collective-permute-done.other), custom_call_target="tpu_custom_call" | custom-call | flops 49999998976 | bytes 1048576 | tf_op jit(solution)/shard_map/spread/pallas_call | solution.py:139
  4.3 10.7 %all_to_all.10.features = bf16[8,4,16,128]{3,2,1,0:T(8,128)(2,1)S(1)} all-to-all(bf16[8,4,16,128]{3,2,1,0:T(8,128)(2,1)S(1)} %spread.1), channel_id=1, replica_groups={{11,13,15,0,2,4,6,9},{10,12,14,1,3,5,7,8},{27,29,31,16,18,20,22,25},{26..., dimensions={0} | all-to-all | bytes 262144 | tf_op jit(solution)/shard_map/all_to_all | solution.py:266
  15.0 0.0 collective-permute-done.1.other
  15.0 0.6 %score.1 = f32[16,2,384]{2,1,0:T(2,128)S(1)} custom-call(bf16[8,4,16,128]{3,2,1,0:T(8,128)(2,1)S(1)} %all_to_all.10.features, bf16[192,4096]{1,0:T(8,128)(2,1)S(1)} %copy-done, bf16[192,4096]{1,0:T(8,128)(2,1)S(1)} %collective-permute-done.1.other), custom_call_target="tpu_custom_call" | custom-call | tf_op jit(solution)/shard_map/score/pallas_call | solution.py:174
  15.7 8.7 %all_to_all.11.scores = f32[16,2,384]{2,1,0:T(2,128)S(1)} all-to-all(f32[16,2,384]{2,1,0:T(2,128)S(1)} %score.1), channel_id=1, replica_groups={{15,0,1,2,3,4,5,6,7,8,9,10,11,12,13,14},{31,16,17,18,19,20,21,22,23,24,..., dimensions={0} | all-to-all | bytes 98304 | tf_op jit(solution)/shard_map/all_to_all | solution.py:271
  24.4 0.7 %pick.1 = f32[3,2,384]{2,1,0:T(2,128)} custom-call(s32[2,6]{1,0:T(2,128)S(4)} %plan.1.table, f32[16,2,384]{2,1,0:T(2,128)S(1)} %all_to_all.11.scores), custom_call_target="tpu_custom_call" | custom-call | tf_op jit(solution)/shard_map/pick/pallas_call | solution.py:234
Async XLA Ops:
  0.0 3.0 %copy-start = (bf16[192,4096]{1,0:T(8,128)(2,1)S(1)}, bf16[192,4096]{1,0:T(8,128)(2,1)}, u32[]{:S(2)}) copy-start(bf16[192,4096]{1,0:T(8,128)(2,1)} %own) | copy-start | bytes 4718596
  0.0 3.1 %copy-start.1 = (s32[6,2]{0,1:T(2,128)S(1)}, s32[6,2]{0,1:T(2,128)}, u32[]{:S(2)}) copy-start(s32[6,2]{0,1:T(2,128)} %param.11) | copy-start | bytes 148
  2.5 1.5 %collective-permute-start = (f32[288,128]{1,0:T(8,128)S(1)}, f32[288,128]{1,0:T(8,128)S(1)}, u32[]{:S(2)}, u32[]{:S(2)}) collective-permute-start(f32[288,128]{1,0:T(8,128)S(1)} %project.1.own), channel_id=1, source_target_pairs={{0,1},{1,0},{2,3},{3,2},{4,5},{5,4},{6,7},{7,6},{8,9},{9,8},{10,11... | collective-permute-start | bytes 442376 | tf_op jit(solution)/shard_map/ppermute | solution.py:255
  3.0 12.0 %collective-permute-start.1 = (bf16[192,4096]{1,0:T(8,128)(2,1)S(1)}, bf16[192,4096]{1,0:T(8,128)(2,1)S(1)}, u32[]{:S(2)}, u32[]{:S(2)}) collective-permute-start(bf16[192,4096]{1,0:T(8,128)(2,1)S(1)} %copy-done), channel_id=1, source_target_pairs={{0,1},{1,0},{2,3},{3,2},{4,5},{5,4},{6,7},{7,6},{8,9},{9,8},{10,11... | collective-permute-start | bytes 4718600 | tf_op jit(solution)/shard_map/ppermute | solution.py:259

commit v11 on v10

--- a/solution.py
+++ b/solution.py
@@ -54,8 +54,8 @@
 def project_kernel(acts, grads, p_in, p_out, out, x_v, w_v, sems):
     proj = p_in.shape[0]
     for side, (x, w) in enumerate(((grads, p_out), (acts, p_in))):
+        pltpu.make_async_copy(x, x_v.at[side], sems.at[side, 1]).start()
         pltpu.make_async_copy(w, w_v.at[side, pl.ds(side * proj, proj)], sems.at[side, 0]).start()
-        pltpu.make_async_copy(x, x_v.at[side], sems.at[side, 1]).start()
     for side in range(2):
         w_v[side, pl.ds((1 - side) * proj, proj)] = jnp.zeros(p_in.shape, w_v.dtype)
     out[...] = jnp.zeros_like(out)

time: 25.3 us -> 25.2 us (level)
  no operation moved by 1% of the time
where the time goes in v11:
time: 25.2 us; the launch traced here: 25 us
  blocking collectives  19.4 us (77%)
  Pallas kernels  4.7 us (19%)
  starting transfers between devices  0.6 us (2%)
  waiting for transfers between devices  0.29 us (1%)
    all_to_all x1, blocking collectives, body(): lax.all_to_all(sent, ('dp', 'tensor'), split_axis=0, concat_axis=0, tiled...  10.7 us
    all_to_all x1, blocking collectives, body(): lax.all_to_all(scores, ('dp', 'tensor'), split_axis=0, concat_axis=0, til...  8.74 us
    pallas_call x1, Pallas kernels, project(): pl.pallas_call(project_kernel, out_shape=jax.ShapeDtypeStruct((rows, 2 *...  2.41 us
    pallas_call x1, Pallas kernels, pick(): pl.pallas_call(functools.partial(pick_kernel, meet), out_shape=jax.ShapeD...  0.67 us
    pallas_call x1, Pallas kernels, score(): pl.pallas_call(functools.partial(score_kernel, meet), out_shape=jax.Shape...  0.64 us
    pallas_call x1, Pallas kernels, plan(): pl.pallas_call(functools.partial(plan_kernel, share, peers, meet), out_sh...  0.62 us
    ppermute x1, starting transfers between devices, body(): other = lax.ppermute(own, 'tensor', swap)  0.52 us
  transfers between devices with their start and end apart: 2, of which 1 were waited for; matrix products, arithmetic and copies ran while one was open for 0% of the time, Pallas kernels for 4%

profile of v11, /device:TPU:0, one launch (start us, length us, event | category | flops | bytes accessed | tf_op | source)
XLA Modules:
  0.0 25.0 jit_solution(6241177939058296708)
XLA Ops:
  0.0 0.0 copy-start
  0.0 0.0 copy-start.1
  0.0 2.4 %project.1.own = f32[288,128]{1,0:T(8,128)S(1)} custom-call(bf16[288,2048]{1,0:T(8,128)(2,1)} %bitcast.6, bf16[288,2048]{1,0:T(8,128)(2,1)} %bitcast.7, bf16[64,2048]{1,0:T(8,128)(2,1)} %bitcast.8, bf16[64,2048]{1,0:T(8,128)(2,1)} %bitcast.9), custom_call_target="tpu_custom_call" | custom-call | tf_op jit(solution)/shard_map/project/pallas_call | solution.py:74
  2.4 0.5 %collective-permute-start = (f32[288,128]{1,0:T(8,128)S(1)}, f32[288,128]{1,0:T(8,128)S(1)}, u32[]{:S(2)}, u32[]{:S(2)}) collective-permute-start(f32[288,128]{1,0:T(8,128)S(1)} %project.1.own), channel_id=1, source_target_pairs={{0,1},{1,0},{2,3},{3,2},{4,5},{5,4},{6,7},{7,6},{8,9},{9,8},{10,11... | collective-permute-start | bytes 442376 | tf_op jit(solution)/shard_map/ppermute | solution.py:255
  2.9 0.0 copy-done
  2.9 0.1 collective-permute-start.1
  3.0 0.0 copy-done.1
  3.0 0.6 %plan.1.table = s32[2,6]{1,0:T(2,128)S(4)} custom-call(s32[2,6]{1,0:T(2,128)S(1)} %bitcast.5, f32[288,128]{1,0:T(8,128)S(1)} %project.1.own), custom_call_target="tpu_custom_call" | custom-call | tf_op jit(solution)/shard_map/plan/pallas_call | solution.py:206
  3.7 0.3 %collective-permute-done.other = f32[288,128]{1,0:T(8,128)S(1)} collective-permute-done((f32[288,128]{1,0:T(8,128)S(1)}, f32[288,128]{1,0:T(8,128)S(1)}, u32[]{:S(2)}, u32[]{:S(2)}) %collective-permute-start) | collective-permute-done | bytes 147488 | tf_op jit(solution)/shard_map/ppermute | solution.py:255
  3.9 0.4 %spread.1 = bf16[8,4,16,128]{3,2,1,0:T(8,128)(2,1)S(1)} custom-call(s32[2,6]{1,0:T(2,128)S(4)} %plan.1.table, f32[288,128]{1,0:T(8,128)S(1)} %project.1.own, f32[288,128]{1,0:T(8,128)S(1)} %collective-permute-done.other), custom_call_target="tpu_custom_call" | custom-call | flops 49999998976 | bytes 1048576 | tf_op jit(solution)/shard_map/spread/pallas_call | solution.py:139
  4.3 10.7 %all_to_all.10.features = bf16[8,4,16,128]{3,2,1,0:T(8,128)(2,1)S(1)} all-to-all(bf16[8,4,16,128]{3,2,1,0:T(8,128)(2,1)S(1)} %spread.1), channel_id=1, replica_groups={{11,13,15,0,2,4,6,9},{10,12,14,1,3,5,7,8},{27,29,31,16,18,20,22,25},{26..., dimensions={0} | all-to-all | bytes 262144 | tf_op jit(solution)/shard_map/all_to_all | solution.py:266
  15.0 0.0 collective-permute-done.1.other
  15.0 0.6 %score.1 = f32[16,2,384]{2,1,0:T(2,128)S(1)} custom-call(bf16[8,4,16,128]{3,2,1,0:T(8,128)(2,1)S(1)} %all_to_all.10.features, bf16[192,4096]{1,0:T(8,128)(2,1)S(1)} %copy-done, bf16[192,4096]{1,0:T(8,128)(2,1)S(1)} %collective-permute-done.1.other), custom_call_target="tpu_custom_call" | custom-call | tf_op jit(solution)/shard_map/score/pallas_call | solution.py:174
  15.6 8.7 %all_to_all.11.scores = f32[16,2,384]{2,1,0:T(2,128)S(1)} all-to-all(f32[16,2,384]{2,1,0:T(2,128)S(1)} %score.1), channel_id=1, replica_groups={{15,0,1,2,3,4,5,6,7,8,9,10,11,12,13,14},{31,16,17,18,19,20,21,22,23,24,..., dimensions={0} | all-to-all | bytes 98304 | tf_op jit(solution)/shard_map/all_to_all | solution.py:271
  24.4 0.7 %pick.1 = f32[3,2,384]{2,1,0:T(2,128)} custom-call(s32[2,6]{1,0:T(2,128)S(4)} %plan.1.table, f32[16,2,384]{2,1,0:T(2,128)S(1)} %all_to_all.11.scores), custom_call_target="tpu_custom_call" | custom-call | tf_op jit(solution)/shard_map/pick/pallas_call | solution.py:234
Async XLA Ops:
  0.0 2.9 %copy-start = (bf16[192,4096]{1,0:T(8,128)(2,1)S(1)}, bf16[192,4096]{1,0:T(8,128)(2,1)}, u32[]{:S(2)}) copy-start(bf16[192,4096]{1,0:T(8,128)(2,1)} %own) | copy-start | bytes 4718596
  0.0 3.0 %copy-start.1 = (s32[6,2]{0,1:T(2,128)S(1)}, s32[6,2]{0,1:T(2,128)}, u32[]{:S(2)}) copy-start(s32[6,2]{0,1:T(2,128)} %param.11) | copy-start | bytes 148
  2.4 1.5 %collective-permute-start = (f32[288,128]{1,0:T(8,128)S(1)}, f32[288,128]{1,0:T(8,128)S(1)}, u32[]{:S(2)}, u32[]{:S(2)}) collective-permute-start(f32[288,128]{1,0:T(8,128)S(1)} %project.1.own), channel_id=1, source_target_pairs={{0,1},{1,0},{2,3},{3,2},{4,5},{5,4},{6,7},{7,6},{8,9},{9,8},{10,11... | collective-permute-start | bytes 442376 | tf_op jit(solution)/shard_map/ppermute | solution.py:255
  2.9 12.0 %collective-permute-start.1 = (bf16[192,4096]{1,0:T(8,128)(2,1)S(1)}, bf16[192,4096]{1,0:T(8,128)(2,1)S(1)}, u32[]{:S(2)}, u32[]{:S(2)}) collective-permute-start(bf16[192,4096]{1,0:T(8,128)(2,1)S(1)} %copy-done), channel_id=1, source_target_pairs={{0,1},{1,0},{2,3},{3,2},{4,5},{5,4},{6,7},{7,6},{8,9},{9,8},{10,11... | collective-permute-start | bytes 4718600 | tf_op jit(solution)/shard_map/ppermute | solution.py:259

commit v12 on v11

--- a/solution.py
+++ b/solution.py
@@ -18,11 +18,11 @@
 
 
 def half_of(index, core, peers):
-    return core ^ (index >= peers // 2)
+    return core ^ (index >= 3 * peers // 4)
 
 
 def my_half(peers):
-    past = (lax.axis_index("dp") >= peers // 2).astype(jnp.int32)
+    past = (lax.axis_index("dp") >= 3 * peers // 4).astype(jnp.int32)
     return lax.axis_index("tensor") ^ past
 
 

time: 25.2 us -> 25.2 us (level)
    all_to_all x1, blocking collectives: 8.74 us -> 8.13 us  [body(): lax.all_to_all(scores, ('dp', 'tensor'), split_axis=0, concat_axis=0, til...]
    all_to_all x1, blocking collectives: 10.7 us -> 11.2 us  [body(): lax.all_to_all(sent, ('dp', 'tensor'), split_axis=0, concat_axis=0, tiled...]
where the time goes in v12:
time: 25.2 us; the launch traced here: 25 us
  blocking collectives  19.3 us (77%)
  Pallas kernels  4.69 us (19%)
  starting transfers between devices  0.6 us (2%)
  waiting for transfers between devices  0.29 us (1%)
    all_to_all x1, blocking collectives, body(): lax.all_to_all(sent, ('dp', 'tensor'), split_axis=0, concat_axis=0, tiled...  11.2 us
    all_to_all x1, blocking collectives, body(): lax.all_to_all(scores, ('dp', 'tensor'), split_axis=0, concat_axis=0, til...  8.13 us
    pallas_call x1, Pallas kernels, project(): pl.pallas_call(project_kernel, out_shape=jax.ShapeDtypeStruct((rows, 2 *...  2.41 us
    pallas_call x1, Pallas kernels, pick(): pl.pallas_call(functools.partial(pick_kernel, meet), out_shape=jax.ShapeD...  0.67 us
    pallas_call x1, Pallas kernels, score(): pl.pallas_call(functools.partial(score_kernel, meet), out_shape=jax.Shape...  0.64 us
    pallas_call x1, Pallas kernels, plan(): pl.pallas_call(functools.partial(plan_kernel, share, peers, meet), out_sh...  0.62 us
    ppermute x1, starting transfers between devices, body(): other = lax.ppermute(own, 'tensor', swap)  0.52 us
  transfers between devices with their start and end apart: 2, of which 1 were waited for; matrix products, arithmetic and copies ran while one was open for 0% of the time, Pallas kernels for 4%

profile of v12, /device:TPU:0, one launch (start us, length us, event | category | flops | bytes accessed | tf_op | source)
XLA Modules:
  0.0 25.0 jit_solution(7290735109840515306)
XLA Ops:
  0.0 0.0 copy-start
  0.0 0.0 copy-start.1
  0.0 2.4 %project.1.own = f32[288,128]{1,0:T(8,128)S(1)} custom-call(bf16[288,2048]{1,0:T(8,128)(2,1)} %bitcast.6, bf16[288,2048]{1,0:T(8,128)(2,1)} %bitcast.7, bf16[64,2048]{1,0:T(8,128)(2,1)} %bitcast.8, bf16[64,2048]{1,0:T(8,128)(2,1)} %bitcast.9), custom_call_target="tpu_custom_call" | custom-call | tf_op jit(solution)/shard_map/project/pallas_call | solution.py:74
  2.4 0.5 %collective-permute-start = (f32[288,128]{1,0:T(8,128)S(1)}, f32[288,128]{1,0:T(8,128)S(1)}, u32[]{:S(2)}, u32[]{:S(2)}) collective-permute-start(f32[288,128]{1,0:T(8,128)S(1)} %project.1.own), channel_id=1, source_target_pairs={{0,1},{1,0},{2,3},{3,2},{4,5},{5,4},{6,7},{7,6},{8,9},{9,8},{10,11... | collective-permute-start | bytes 442376 | tf_op jit(solution)/shard_map/ppermute | solution.py:255
  2.9 0.0 copy-done
  2.9 0.1 collective-permute-start.1
  3.0 0.0 copy-done.1
  3.0 0.6 %plan.1.table = s32[2,6]{1,0:T(2,128)S(4)} custom-call(s32[2,6]{1,0:T(2,128)S(1)} %bitcast.5, f32[288,128]{1,0:T(8,128)S(1)} %project.1.own), custom_call_target="tpu_custom_call" | custom-call | tf_op jit(solution)/shard_map/plan/pallas_call | solution.py:206
  3.7 0.3 %collective-permute-done.other = f32[288,128]{1,0:T(8,128)S(1)} collective-permute-done((f32[288,128]{1,0:T(8,128)S(1)}, f32[288,128]{1,0:T(8,128)S(1)}, u32[]{:S(2)}, u32[]{:S(2)}) %collective-permute-start) | collective-permute-done | bytes 147488 | tf_op jit(solution)/shard_map/ppermute | solution.py:255
  3.9 0.4 %spread.1 = bf16[8,4,16,128]{3,2,1,0:T(8,128)(2,1)S(1)} custom-call(s32[2,6]{1,0:T(2,128)S(4)} %plan.1.table, f32[288,128]{1,0:T(8,128)S(1)} %project.1.own, f32[288,128]{1,0:T(8,128)S(1)} %collective-permute-done.other), custom_call_target="tpu_custom_call" | custom-call | flops 49999998976 | bytes 1048576 | tf_op jit(solution)/shard_map/spread/pallas_call | solution.py:139
  4.3 11.2 %all_to_all.10.features = bf16[8,4,16,128]{3,2,1,0:T(8,128)(2,1)S(1)} all-to-all(bf16[8,4,16,128]{3,2,1,0:T(8,128)(2,1)S(1)} %spread.1), channel_id=1, replica_groups={{10,13,15,0,2,4,6,8},{11,12,14,1,3,5,7,9},{26,29,31,16,18,20,22,24},{27..., dimensions={0} | all-to-all | bytes 262144 | tf_op jit(solution)/shard_map/all_to_all | solution.py:266
  15.5 0.0 collective-permute-done.1.other
  15.5 0.6 %score.1 = f32[16,2,384]{2,1,0:T(2,128)S(1)} custom-call(bf16[8,4,16,128]{3,2,1,0:T(8,128)(2,1)S(1)} %all_to_all.10.features, bf16[192,4096]{1,0:T(8,128)(2,1)S(1)} %copy-done, bf16[192,4096]{1,0:T(8,128)(2,1)S(1)} %collective-permute-done.1.other), custom_call_target="tpu_custom_call" | custom-call | tf_op jit(solution)/shard_map/score/pallas_call | solution.py:174
  16.2 8.1 %all_to_all.11.scores = f32[16,2,384]{2,1,0:T(2,128)S(1)} all-to-all(f32[16,2,384]{2,1,0:T(2,128)S(1)} %score.1), channel_id=1, replica_groups={{15,0,1,2,3,4,5,6,7,8,9,10,11,12,13,14},{31,16,17,18,19,20,21,22,23,24,..., dimensions={0} | all-to-all | bytes 98304 | tf_op jit(solution)/shard_map/all_to_all | solution.py:271
  24.3 0.7 %pick.1 = f32[3,2,384]{2,1,0:T(2,128)} custom-call(s32[2,6]{1,0:T(2,128)S(4)} %plan.1.table, f32[16,2,384]{2,1,0:T(2,128)S(1)} %all_to_all.11.scores), custom_call_target="tpu_custom_call" | custom-call | tf_op jit(solution)/shard_map/pick/pallas_call | solution.py:234
Async XLA Ops:
  0.0 2.9 %copy-start = (bf16[192,4096]{1,0:T(8,128)(2,1)S(1)}, bf16[192,4096]{1,0:T(8,128)(2,1)}, u32[]{:S(2)}) copy-start(bf16[192,4096]{1,0:T(8,128)(2,1)} %own) | copy-start | bytes 4718596
  0.0 3.0 %copy-start.1 = (s32[6,2]{0,1:T(2,128)S(1)}, s32[6,2]{0,1:T(2,128)}, u32[]{:S(2)}) copy-start(s32[6,2]{0,1:T(2,128)} %param.11) | copy-start | bytes 148
  2.4 1.5 %collective-permute-start = (f32[288,128]{1,0:T(8,128)S(1)}, f32[288,128]{1,0:T(8,128)S(1)}, u32[]{:S(2)}, u32[]{:S(2)}) collective-permute-start(f32[288,128]{1,0:T(8,128)S(1)} %project.1.own), channel_id=1, source_target_pairs={{0,1},{1,0},{2,3},{3,2},{4,5},{5,4},{6,7},{7,6},{8,9},{9,8},{10,11... | collective-permute-start | bytes 442376 | tf_op jit(solution)/shard_map/ppermute | solution.py:255
  2.9 12.6 %collective-permute-start.1 = (bf16[192,4096]{1,0:T(8,128)(2,1)S(1)}, bf16[192,4096]{1,0:T(8,128)(2,1)S(1)}, u32[]{:S(2)}, u32[]{:S(2)}) collective-permute-start(bf16[192,4096]{1,0:T(8,128)(2,1)S(1)} %copy-done), channel_id=1, source_target_pairs={{0,1},{1,0},{2,3},{3,2},{4,5},{5,4},{6,7},{7,6},{8,9},{9,8},{10,11... | collective-permute-start | bytes 4718600 | tf_op jit(solution)/shard_map/ppermute | solution.py:259
